TPU v7x, 32 devices: a whole 2x2x4 slice. The times are simulated.
32 devices in a mesh: dp: 8 (over z, y), frames: 4 (over x, core).
Axes of the slice: x: 2, y: 2, z: 4, core: 2. Of those that a mesh axis runs over, the one named last changes fastest.
Arguments:
- tokens: float32 [32, 128, 1024], P(('dp', 'frames')), may hold values from -6 to 6
- memory: bfloat16 [32, 1504, 1024], P('dp', 'frames'), may hold values from -6 to 6
- cotangent: float32 [32, 128, 1024], P(('dp', 'frames')), may hold values from -6 to 6
- self_project: bfloat16 [1024, 3072], P(('dp', 'frames')), may hold values from -0.1875 to 0.1875
- self_output: bfloat16 [1024, 1024], P(('dp', 'frames')), may hold values from -1 to 1
- cross_query: bfloat16 [1024, 1024], P(('dp', 'frames')), may hold values from -0.1875 to 0.1875
- cross_memory: bfloat16 [1024, 2048], P(('dp', 'frames')), may hold values from -0.1875 to 0.1875
- cross_output: bfloat16 [1024, 1024], P(('dp', 'frames')), may hold values from -3.5 to 3.5
- expand: bfloat16 [1024, 4096], P(('dp', 'frames')), may hold values from -0.1875 to 0.1875
- contract: bfloat16 [4096, 1024], P(('dp', 'frames')), may hold values from -0.09375 to 0.09375
- norm_gains: bfloat16 [4, 1024], P(None, ('dp', 'frames')), may hold values from 0.25 to 1.75
- norm_shifts: bfloat16 [4, 1024], P(None, ('dp', 'frames')), may hold values from -1.5 to 1.5
- target_length: int32 [32], P(('dp', 'frames')), may hold values from 42 to 128, as said below
- memory_length: int32 [32], P('dp'), may hold values from 100 to 1504, as said below
- cross_mask: int32 [32, 1504], P('dp'), may hold values 0 or 1
Outputs:
- result: float32 [32, 128, 1024], P(('dp', 'frames'))
- tokens_grad: float32 [32, 128, 1024], P(('dp', 'frames'))
- memory_grad: float32 [32, 1504, 1024], P('dp', 'frames')
- self_project_grad: float32 [1024, 3072], P(('dp', 'frames'))
- self_output_grad: float32 [1024, 1024], P(('dp', 'frames'))
- cross_query_grad: float32 [1024, 1024], P(('dp', 'frames'))
- cross_memory_grad: float32 [1024, 2048], P(('dp', 'frames'))
- cross_output_grad: float32 [1024, 1024], P(('dp', 'frames'))
- expand_grad: float32 [1024, 4096], P(('dp', 'frames'))
- contract_grad: float32 [4096, 1024], P(('dp', 'frames'))
- norm_gains_grad: float32 [4, 1024], P(None, ('dp', 'frames'))
- norm_shifts_grad: float32 [4, 1024], P(None, ('dp', 'frames'))
- branch_rms: float32 [4], replicated
Inputs may be any that keep to these rules, and one draw needn't show every extreme that they name: `target_length`: in every draw some sequence has all 128 rows. `memory_length`: in every group of 4 consecutive items one item has all 1504 frames.
All inputs are finite; a program needn't handle non-finite values. No bound on the sum of `cross_mask` on one device may be relied on, other than what follows from the above.
Results may differ from a plain program's by a relative error of at most 0.029.
Values may be sent and summed in bfloat16 or wider, within the bound.
A program may use at most 192 MiB of HBM per device.

v0:
```python
import jax
import jax.numpy as jnp
from jax import lax
from jax.sharding import PartitionSpec as P

HEAD_DIM = 64


block_heads = 4


def layer_norm(values, gain_row, shift_row):
    center = values - jnp.mean(values, axis=-1, keepdims=True)
    spread = jnp.mean(center * center, axis=-1, keepdims=True)
    return center * lax.rsqrt(spread + 1e-05) * gain_row + shift_row


def exact_gelu(values):
    return jax.nn.gelu(values, approximate=False)


def matmul(left_side, right_side):
    return jnp.dot(left_side, right_side, preferred_element_type=jnp.float32)


def split_heads(rows):
    return rows.reshape(rows.shape[:-1] + (rows.shape[-1] // HEAD_DIM, HEAD_DIM))


def to_blocks(rows):
    row_count, head_count, head_width = rows.shape
    return rows.reshape(row_count, head_count // block_heads, block_heads, head_width).transpose(
        1, 0, 2, 3
    )


def from_blocks(blocks):
    group_count, row_count, head_count, head_width = blocks.shape
    return blocks.transpose(1, 0, 2, 3).reshape(row_count, group_count * head_count * head_width)


def block_scores(query_block, key_block, allowed):
    factor = query_block.shape[-1] ** (-0.5)
    raw_scores = (
        jnp.einsum("shd,fhd->hsf", query_block, key_block, preferred_element_type=jnp.float32)
        * factor
    )
    return jnp.where(allowed[None], raw_scores, -1e30)


def block_probs(query_block, key_block, allowed, max_block, total_block):
    scores = block_scores(query_block, key_block, allowed)
    shifted = jnp.where(allowed[None], jnp.exp(scores - max_block[..., None]), 0.0)
    return shifted / total_block[..., None]


def block_grads(query_block, key_block, grad_block, probs, grad_probs, row_dot):
    factor = query_block.shape[-1] ** (-0.5)
    score_grad = (probs * (grad_probs - row_dot)).astype(jnp.bfloat16)
    query_grad = (
        jnp.einsum("hsf,fhd->shd", score_grad, key_block, preferred_element_type=jnp.float32)
        * factor
    )
    key_grad = (
        jnp.einsum("hsf,shd->fhd", score_grad, query_block, preferred_element_type=jnp.float32)
        * factor
    )
    value_grad = jnp.einsum(
        "hsf,shd->fhd", probs.astype(jnp.bfloat16), grad_block, preferred_element_type=jnp.float32
    )
    return (query_grad, key_grad, value_grad)


def attend_whole(query_rows, key_rows, value_rows, allowed):

    def one_group(blocks):
        query_block, key_block, value_block = blocks
        scores = block_scores(query_block, key_block, allowed)
        max_block = jnp.max(scores, axis=-1)
        shifted = jnp.where(allowed[None], jnp.exp(scores - max_block[..., None]), 0.0)
        total_block = jnp.sum(shifted, axis=-1)
        weights = (shifted / total_block[..., None]).astype(jnp.bfloat16)
        mixture = jnp.einsum(
            "hsf,fhd->shd", weights, value_block, preferred_element_type=jnp.float32
        )
        return (mixture, max_block, total_block)

    mixture, row_max, totals = lax.map(
        one_group, (to_blocks(query_rows), to_blocks(key_rows), to_blocks(value_rows))
    )
    return (from_blocks(mixture), row_max, totals)


def attend_whole_back(query_rows, key_rows, value_rows, allowed, grad_rows, row_max, totals):

    def one_group(blocks):
        query_block, key_block, value_block, grad_block, max_block, total_block = blocks
        probs = block_probs(query_block, key_block, allowed, max_block, total_block)
        grad_probs = jnp.einsum(
            "shd,fhd->hsf", grad_block, value_block, preferred_element_type=jnp.float32
        )
        row_dot = jnp.sum(probs * grad_probs, axis=-1, keepdims=True)
        return block_grads(query_block, key_block, grad_block, probs, grad_probs, row_dot)

    query_grad, key_grad, value_grad = lax.map(
        one_group,
        (
            to_blocks(query_rows),
            to_blocks(key_rows),
            to_blocks(value_rows),
            to_blocks(grad_rows),
            row_max,
            totals,
        ),
    )
    return (from_blocks(query_grad), from_blocks(key_grad), from_blocks(value_grad))


def cross_stats(query_rows, key_rows, allowed):

    def one_group(blocks):
        query_block, key_block = blocks
        scores = block_scores(query_block, key_block, allowed)
        max_block = jnp.max(scores, axis=-1)
        total_block = jnp.sum(
            jnp.where(allowed[None], jnp.exp(scores - max_block[..., None]), 0.0), axis=-1
        )
        return (max_block, total_block)

    return lax.map(one_group, (to_blocks(query_rows), to_blocks(key_rows)))


def cross_partial(query_rows, key_rows, value_rows, allowed, row_max, totals):

    def one_group(blocks):
        query_block, key_block, value_block, max_block, total_block = blocks
        probs = block_probs(query_block, key_block, allowed, max_block, total_block)
        return jnp.einsum(
            "hsf,fhd->shd",
            probs.astype(jnp.bfloat16),
            value_block,
            preferred_element_type=jnp.float32,
        )

    return from_blocks(
        lax.map(
            one_group,
            (to_blocks(query_rows), to_blocks(key_rows), to_blocks(value_rows), row_max, totals),
        )
    )


def cross_row_dot(query_rows, key_rows, value_rows, allowed, grad_rows, row_max, totals):

    def one_group(blocks):
        query_block, key_block, value_block, grad_block, max_block, total_block = blocks
        probs = block_probs(query_block, key_block, allowed, max_block, total_block)
        grad_probs = jnp.einsum(
            "shd,fhd->hsf", grad_block, value_block, preferred_element_type=jnp.float32
        )
        return jnp.sum(probs * grad_probs, axis=-1)

    return lax.map(
        one_group,
        (
            to_blocks(query_rows),
            to_blocks(key_rows),
            to_blocks(value_rows),
            to_blocks(grad_rows),
            row_max,
            totals,
        ),
    )


def cross_partial_grads(
    query_rows, key_rows, value_rows, allowed, grad_rows, row_max, totals, row_dot
):

    def one_group(blocks):
        query_block, key_block, value_block, grad_block, max_block, total_block, dot_block = blocks
        probs = block_probs(query_block, key_block, allowed, max_block, total_block)
        grad_probs = jnp.einsum(
            "shd,fhd->hsf", grad_block, value_block, preferred_element_type=jnp.float32
        )
        return block_grads(
            query_block, key_block, grad_block, probs, grad_probs, dot_block[..., None]
        )

    query_grad, key_grad, value_grad = lax.map(
        one_group,
        (
            to_blocks(query_rows),
            to_blocks(key_rows),
            to_blocks(value_rows),
            to_blocks(grad_rows),
            row_max,
            totals,
            row_dot,
        ),
    )
    return (from_blocks(query_grad), from_blocks(key_grad), from_blocks(value_grad))


def local(
    tokens,
    memory,
    cotangent,
    self_project,
    self_output,
    cross_query,
    cross_memory,
    cross_output,
    expand,
    contract,
    norm_gains,
    norm_shifts,
    target_length,
    memory_length,
    cross_mask,
):
    gathered = (
        lax.all_gather(self_project, ("dp", "frames"), axis=0, tiled=True),
        lax.all_gather(self_output, ("dp", "frames"), axis=0, tiled=True),
        lax.all_gather(cross_query, ("dp", "frames"), axis=0, tiled=True),
        lax.all_gather(cross_memory, ("dp", "frames"), axis=0, tiled=True),
        lax.all_gather(cross_output, ("dp", "frames"), axis=0, tiled=True),
        lax.all_gather(expand, ("dp", "frames"), axis=0, tiled=True),
        lax.all_gather(contract, ("dp", "frames"), axis=0, tiled=True),
        lax.all_gather(norm_gains, ("dp", "frames"), axis=1, tiled=True),
        lax.all_gather(norm_shifts, ("dp", "frames"), axis=1, tiled=True),
    )
    (
        w_self,
        w_self_out,
        w_query,
        w_memory,
        w_cross_out,
        w_expand,
        w_contract,
        gains_low,
        shifts_low,
    ) = gathered
    gains = gains_low.astype(jnp.float32)
    shifts = shifts_low.astype(jnp.float32)
    model_width = w_self_out.shape[0]
    residual_in = tokens[0]
    length = residual_in.shape[0]
    positions = jnp.arange(length)
    row_valid = positions < target_length[0]
    causal = positions[:, None] >= positions[None, :]
    item_count = memory.shape[0]
    frame_count = memory.shape[1]
    own_item = lax.axis_index("frames")
    normed_one_f, back_one = jax.vjp(layer_norm, residual_in, gains[0], shifts[0])
    normed_one = normed_one_f.astype(jnp.bfloat16)
    joint_rows = matmul(normed_one, w_self).astype(jnp.bfloat16)
    self_queries = split_heads(joint_rows[:, :model_width])
    self_keys = split_heads(joint_rows[:, model_width : 2 * model_width])
    self_values = split_heads(joint_rows[:, 2 * model_width :])
    self_mix, self_max, self_totals = attend_whole(self_queries, self_keys, self_values, causal)
    self_mix_low = self_mix.astype(jnp.bfloat16)
    self_branch = matmul(self_mix_low, w_self_out)
    first_sum = residual_in + self_branch
    normed_two_f, back_two = jax.vjp(layer_norm, first_sum, gains[1], shifts[1])
    normed_two = normed_two_f.astype(jnp.bfloat16)
    cross_queries = matmul(normed_two, w_query).astype(jnp.bfloat16)
    every_query = lax.all_gather(cross_queries[None], "frames", axis=0, tiled=True)
    query_heads = split_heads(every_query)
    frame_start = own_item * frame_count
    local_frames = frame_start + jnp.arange(frame_count)
    local_mask = lax.dynamic_slice_in_dim(cross_mask, frame_start, frame_count, 1)
    frame_ok = (local_frames[None, :] < memory_length[:, None]) & (
        (local_mask == 1) | (local_frames[None, :] == 0)
    )
    memory_rows = matmul(memory.reshape(item_count * frame_count, model_width), w_memory).astype(
        jnp.bfloat16
    )
    memory_rows = memory_rows.reshape(item_count, frame_count, 2 * model_width)
    memory_keys = split_heads(memory_rows[..., :model_width])
    memory_values = split_heads(memory_rows[..., model_width:])

    def item_stats(inputs):
        query_item, key_item, frame_item = inputs
        return cross_stats(
            query_item, key_item, jnp.broadcast_to(frame_item[None, :], (length, frame_count))
        )

    local_max, local_totals = lax.map(item_stats, (query_heads, memory_keys, frame_ok))
    cross_max = lax.pmax(local_max.astype(jnp.bfloat16), "frames").astype(local_max.dtype)
    cross_totals = lax.psum(
        (local_totals * jnp.exp(local_max - cross_max)).astype(jnp.bfloat16), "frames"
    ).astype(jnp.float32)

    def item_partial(inputs):
        query_item, key_item, value_item, frame_item, max_item, total_item = inputs
        allowed = jnp.broadcast_to(frame_item[None, :], (length, frame_count))
        return cross_partial(query_item, key_item, value_item, allowed, max_item, total_item)

    partial_mix = lax.map(
        item_partial, (query_heads, memory_keys, memory_values, frame_ok, cross_max, cross_totals)
    )
    cross_mix = lax.psum_scatter(
        partial_mix.astype(jnp.bfloat16), "frames", scatter_dimension=0, tiled=True
    ).astype(jnp.float32)[0]
    cross_mix_low = cross_mix.astype(jnp.bfloat16)
    cross_branch = matmul(cross_mix_low, w_cross_out)
    second_sum = first_sum + cross_branch
    normed_three_f, back_three = jax.vjp(layer_norm, second_sum, gains[2], shifts[2])
    normed_three = normed_three_f.astype(jnp.bfloat16)
    hidden = matmul(normed_three, w_expand)
    active_f, gelu_back = jax.vjp(exact_gelu, hidden)
    active = active_f.astype(jnp.bfloat16)
    feed_branch = matmul(active, w_contract)
    third_sum = second_sum + feed_branch
    final_rows, back_final = jax.vjp(layer_norm, third_sum, gains[3], shifts[3])
    result = jnp.where(row_valid[:, None], final_rows, 0.0)
    row_weight = row_valid.astype(jnp.float32)[:, None]
    squares = jnp.stack(
        [
            jnp.sum(row_weight * member * member)
            for member in (third_sum, self_branch, cross_branch, feed_branch)
        ]
    )
    squares_all, counted = lax.psum((squares, jnp.sum(row_weight)), ("dp", "frames"))
    branch_rms = jnp.sqrt(squares_all / (counted * model_width))
    grad_result = jnp.where(row_valid[:, None], cotangent[0], 0.0)
    grad_third, gain_grad_three, shift_grad_three = back_final(grad_result)
    feed_low = grad_third.astype(jnp.bfloat16)
    contract_grad = matmul(active.T, feed_low)
    grad_active = matmul(feed_low, w_contract.T)
    grad_hidden = gelu_back(grad_active)[0].astype(jnp.bfloat16)
    expand_grad = matmul(normed_three.T, grad_hidden)
    grad_normed_three = matmul(grad_hidden, w_expand.T)
    grad_second_part, gain_grad_two, shift_grad_two = back_three(grad_normed_three)
    grad_second = grad_third + grad_second_part
    cross_low = grad_second.astype(jnp.bfloat16)
    cross_output_grad = matmul(cross_mix_low.T, cross_low)
    grad_cross_mix = matmul(cross_low, w_cross_out.T).astype(jnp.bfloat16)
    every_grad = split_heads(lax.all_gather(grad_cross_mix[None], "frames", axis=0, tiled=True))

    def item_dot(inputs):
        query_item, key_item, value_item, frame_item, grad_item, max_item, total_item = inputs
        allowed = jnp.broadcast_to(frame_item[None, :], (length, frame_count))
        return cross_row_dot(
            query_item, key_item, value_item, allowed, grad_item, max_item, total_item
        )

    local_dot = lax.map(
        item_dot,
        (query_heads, memory_keys, memory_values, frame_ok, every_grad, cross_max, cross_totals),
    )
    row_dot = lax.psum(local_dot.astype(jnp.bfloat16), "frames").astype(jnp.float32)

    def item_grads(inputs):
        query_item, key_item, value_item, frame_item, grad_item, max_item, total_item, dot_item = (
            inputs
        )
        allowed = jnp.broadcast_to(frame_item[None, :], (length, frame_count))
        return cross_partial_grads(
            query_item, key_item, value_item, allowed, grad_item, max_item, total_item, dot_item
        )

    query_parts, key_parts, value_parts = lax.map(
        item_grads,
        (
            query_heads,
            memory_keys,
            memory_values,
            frame_ok,
            every_grad,
            cross_max,
            cross_totals,
            row_dot,
        ),
    )
    query_grad = lax.psum_scatter(
        query_parts.astype(jnp.bfloat16), "frames", scatter_dimension=0, tiled=True
    ).astype(jnp.float32)[0]
    memory_low = (
        jnp.concatenate([key_parts, value_parts], axis=2)
        .astype(jnp.bfloat16)
        .reshape(item_count * frame_count, 2 * model_width)
    )
    cross_memory_grad = matmul(memory.reshape(item_count * frame_count, model_width).T, memory_low)
    memory_grad = matmul(memory_low, w_memory.T).reshape(item_count, frame_count, model_width)
    query_low = query_grad.astype(jnp.bfloat16)
    cross_query_grad = matmul(normed_two.T, query_low)
    grad_normed_two = matmul(query_low, w_query.T)
    grad_first_part, gain_grad_one, shift_grad_one = back_two(grad_normed_two)
    grad_first = grad_second + grad_first_part
    self_low = grad_first.astype(jnp.bfloat16)
    self_output_grad = matmul(self_mix_low.T, self_low)
    grad_self_mix = matmul(self_low, w_self_out.T).astype(jnp.bfloat16)
    self_query_grad, self_key_grad, self_value_grad = attend_whole_back(
        self_queries,
        self_keys,
        self_values,
        causal,
        split_heads(grad_self_mix),
        self_max,
        self_totals,
    )
    joint_grad = jnp.concatenate([self_query_grad, self_key_grad, self_value_grad], axis=1).astype(
        jnp.bfloat16
    )
    self_project_grad = matmul(normed_one.T, joint_grad)
    grad_normed_one = matmul(joint_grad, w_self.T)
    grad_input_part, gain_grad_zero, shift_grad_zero = back_one(grad_normed_one)
    tokens_grad = grad_first + grad_input_part
    gain_grads = jnp.stack([gain_grad_zero, gain_grad_one, gain_grad_two, gain_grad_three])
    shift_grads = jnp.stack([shift_grad_zero, shift_grad_one, shift_grad_two, shift_grad_three])
    reduced = (
        lax.psum_scatter(self_project_grad, ("dp", "frames"), scatter_dimension=0, tiled=True),
        lax.psum_scatter(self_output_grad, ("dp", "frames"), scatter_dimension=0, tiled=True),
        lax.psum_scatter(cross_query_grad, ("dp", "frames"), scatter_dimension=0, tiled=True),
        lax.psum_scatter(cross_memory_grad, ("dp", "frames"), scatter_dimension=0, tiled=True),
        lax.psum_scatter(cross_output_grad, ("dp", "frames"), scatter_dimension=0, tiled=True),
        lax.psum_scatter(expand_grad, ("dp", "frames"), scatter_dimension=0, tiled=True),
        lax.psum_scatter(contract_grad, ("dp", "frames"), scatter_dimension=0, tiled=True),
        lax.psum_scatter(gain_grads, ("dp", "frames"), scatter_dimension=1, tiled=True),
        lax.psum_scatter(shift_grads, ("dp", "frames"), scatter_dimension=1, tiled=True),
    )
    (
        project_part,
        output_part,
        query_part,
        memory_part,
        cross_out_part,
        expand_part,
        contract_part,
        gains_part,
        shifts_part,
    ) = reduced
    return (
        result[None],
        tokens_grad[None],
        memory_grad,
        project_part,
        output_part,
        query_part,
        memory_part,
        cross_out_part,
        expand_part,
        contract_part,
        gains_part,
        shifts_part,
        branch_rms,
    )


def solution(mesh):
    return jax.shard_map(
        local,
        mesh=mesh,
        in_specs=(
            P(("dp", "frames"), None, None),
            P("dp", "frames", None),
            P(("dp", "frames"), None, None),
            P(("dp", "frames"), None),
            P(("dp", "frames"), None),
            P(("dp", "frames"), None),
            P(("dp", "frames"), None),
            P(("dp", "frames"), None),
            P(("dp", "frames"), None),
            P(("dp", "frames"), None),
            P(None, ("dp", "frames")),
            P(None, ("dp", "frames")),
            P(("dp", "frames")),
            P("dp"),
            P("dp", None),
        ),
        out_specs=(
            P(("dp", "frames"), None, None),
            P(("dp", "frames"), None, None),
            P("dp", "frames", None),
            P(("dp", "frames"), None),
            P(("dp", "frames"), None),
            P(("dp", "frames"), None),
            P(("dp", "frames"), None),
            P(("dp", "frames"), None),
            P(("dp", "frames"), None),
            P(("dp", "frames"), None),
            P(None, ("dp", "frames")),
            P(None, ("dp", "frames")),
            P(),
        ),
        check_vma=False,
    )
```

profile of v0, /device:TPU:0, one launch (start us, length us, event | category | flops | bytes accessed | tf_op | source)
XLA Modules:
  0.0 2335.9 jit_solution(10782717001738505222)
XLA Ops:
  10.1 43.6 %all-gather.2 = bf16[32,32,4]{1,2,0:T(4,128)(2,1)S(1)} all-gather(bf16[1,32,4]{1,2,0:T(4,128)(2,1)} %bitcast.584), channel_id=1, replica_groups=mesh['dp'=8,'frames'=4] {'dp','frames'}, dimensions={0}, use_global_device_ids=true | all-gather | bytes 8448 | tf_op jit(solution)/shard_map/all_gather | solution.py:230
  53.7 37.2 %all-gather.3 = bf16[32,32,4]{1,2,0:T(4,128)(2,1)S(1)} all-gather(bf16[1,32,4]{1,2,0:T(4,128)(2,1)} %bitcast.585), channel_id=1, replica_groups=mesh['dp'=8,'frames'=4] {'dp','frames'}, dimensions={0}, use_global_device_ids=true | all-gather | bytes 8448 | tf_op jit(solution)/shard_map/all_gather | solution.py:231
  104.1 13.8 while.136
  117.8 23.3 all-gather.16.cloned.1.call-done
  145.2 54.1 %all-gather.18.cloned.1.call-done = bf16[1024,1024]{1,0:T(8,128)(2,1)} async-done(((bf16[32,1024]{1,0:T(8,128)(2,1)}), bf16[1024,1024]{1,0:T(8,128)(2,1)}) %all-gather.18.cloned.1.call-update) | async-done | bytes 2097168 | tf_op jit(solution)/shard_map/all_gather | solution.py:225
  203.8 59.2 %all-gather.20.cloned.1.call-done = bf16[1024,2048]{1,0:T(8,128)(2,1)} async-done(((bf16[32,2048]{1,0:T(8,128)(2,1)}), bf16[1024,2048]{1,0:T(8,128)(2,1)}) %all-gather.20.cloned.1.call-update) | async-done | bytes 4194320 | tf_op jit(solution)/shard_map/all_gather | solution.py:226
  292.3 37.6 %while.129 = (s32[]{:T(128)}, f32[4,4,4,128]{3,2,1,0:T(4,128)S(1)}, f32[4,4,4,128]{3,2,1,0:T(4,128)S(1)}, bf16[4,128,16,64]{1,3,2,0:T(8,128)(2,1)}, bf16[4,376,1...) while((s32[]{:T(128)}, f32[4,4,4,128]{3,2,1,0:T(4,128)S(1)}, ...), condition=%wide.region_13.14_spmd, body=%wide.region_8.13_spmd.sunk | while | flops 25795584 | bytes 3916646 | solution.py:289
  352.7 58.3 %while.131 = (s32[]{:T(128)}, bf16[4,128,1024]{1,2,0:T(8,128)(2,1)}, bf16[4,128,16,64]{1,3,2,0:T(8,128)(2,1)}, bf16[4,376,16,64]{1,3,2,0:T(8,128)(2,1)}, bf16[4,...) while((s32[]{:T(128)}, bf16[4,128,1024]{1,2,0:T(8,128)(2,1)}, ...), condition=%wide.region_19.20_spmd, body=%wide.region_16.19_spmd.sunk | while | flops 50438144 | bytes 4767774 | solution.py:300
  413.7 21.2 reduce-scatter.18.cloned.1.call-done
  438.9 76.7 %all-gather.24.cloned.1.call-done = bf16[1024,4096]{1,0:T(8,128)(2,1)} async-done(((bf16[32,4096]{1,0:T(8,128)(2,1)}), bf16[1024,4096]{1,0:T(8,128)(2,1)}) %all-gather.24.cloned.1.call-update) | async-done | bytes 8388624 | tf_op jit(solution)/shard_map/all_gather | solution.py:228
  525.2 69.8 %all-gather.26.cloned.1.call-done = bf16[4096,1024]{1,0:T(8,128)(2,1)} async-done(((bf16[128,1024]{1,0:T(8,128)(2,1)}), bf16[4096,1024]{1,0:T(8,128)(2,1)}) %all-gather.26.cloned.1.call-update) | async-done | bytes 8388624 | tf_op jit(solution)/shard_map/all_gather | solution.py:229
  615.5 15.2 all-gather.30.cloned.1.call-done
  638.3 63.0 %while.133 = (s32[]{:T(128)}, bf16[4,4,4,128]{3,2,1,0:T(4,128)(2,1)S(1)}, bf16[4,128,16,64]{1,3,2,0:T(8,128)(2,1)}, bf16[4,376,16,64]{1,3,2,0:T(8,128)(2,1)}, bf...) while((s32[]{:T(128)}, ...), condition=%wide.region_33.34_spmd, body=%wide.region_29.33_spmd.sunk | while | flops 50630144 | bytes 6252982 | solution.py:349
  712.7 182.1 %while.135 = (s32[]{:T(128)}, bf16[4,128,1024]{1,2,0:T(8,128)(2,1)}, bf16[4,376,1024]{2,1,0:T(8,128)(2,1)}, bf16[4,376,1024]{2,1,0:T(8,128)(2,1)}, bf16[4,128,16...) while((s32[]{:T(128)}, bf16[4,128,1024]{1,2,0:T(8,128)(2,1)}, ...), condition=%wide.region_38.39_spmd, body=%wide.region_35.38_spmd.sunk | while | flops 125069312 | bytes 28444780 | solution.py:364
  717.3 30.6 %while.141 = (s32[]{:T(128)}, bf16[4,128,4,64]{1,3,2,0:T(8,128)(2,1)}, bf16[4,376,4,64]{1,3,2,0:T(8,128)(2,1)}, bf16[4,376,4,64]{1,3,2,0:T(8,128)(2,1)}, bf16[4,...) while((s32[]{:T(128)}, ...), condition=%wide.region_37.37_spmd.clone, body=%wide.region_36.36_spmd.clone.sunk | while | flops 125069312 | bytes 17579628 | solution.py:190
  762.8 30.6 %while.141 = (s32[]{:T(128)}, bf16[4,128,4,64]{1,3,2,0:T(8,128)(2,1)}, bf16[4,376,4,64]{1,3,2,0:T(8,128)(2,1)}, bf16[4,376,4,64]{1,3,2,0:T(8,128)(2,1)}, bf16[4,...) while((s32[]{:T(128)}, ...), condition=%wide.region_37.37_spmd.clone, body=%wide.region_36.36_spmd.clone.sunk | while | flops 125069312 | bytes 17579628 | solution.py:190
  808.4 30.6 %while.141 = (s32[]{:T(128)}, bf16[4,128,4,64]{1,3,2,0:T(8,128)(2,1)}, bf16[4,376,4,64]{1,3,2,0:T(8,128)(2,1)}, bf16[4,376,4,64]{1,3,2,0:T(8,128)(2,1)}, bf16[4,...) while((s32[]{:T(128)}, ...), condition=%wide.region_37.37_spmd.clone, body=%wide.region_36.36_spmd.clone.sunk | while | flops 125069312 | bytes 17579628 | solution.py:190
  853.9 30.6 %while.141 = (s32[]{:T(128)}, bf16[4,128,4,64]{1,3,2,0:T(8,128)(2,1)}, bf16[4,376,4,64]{1,3,2,0:T(8,128)(2,1)}, bf16[4,376,4,64]{1,3,2,0:T(8,128)(2,1)}, bf16[4,...) while((s32[]{:T(128)}, ...), condition=%wide.region_37.37_spmd.clone, body=%wide.region_36.36_spmd.clone.sunk | while | flops 125069312 | bytes 17579628 | solution.py:190
  894.9 26.0 %reduce-scatter.20.cloned.1.call-done = bf16[1,128,1024]{1,2,0:T(8,128)(2,1)} async-done(((bf16[4,128,1024]{1,2,0:T(8,128)(2,1)}), bf16[1,128,1024]{1,2,0:T(8,128)(2,1)}) %reduce-scatter.20.cloned.1.call-update) | async-done | bytes 262160 | tf_op jit(solution)/shard_map/reduce_scatter | solution.py:377
  931.2 27.2 %while.137 = (s32[]{:T(128)}, bf16[4,128,4,64]{1,3,2,0:T(8,128)(2,1)}, bf16[4,128,4,64]{1,3,2,0:T(8,128)(2,1)}, bf16[4,128,4,64]{1,3,2,0:T(8,128)(2,1)}, bf16[4,...) while((s32[]{:T(128)}, ...), condition=%wide.region_44.45_spmd.clone.clone, body=%wide.region_42.44_spmd.clone.clone.sunk | while | flops 42745344 | bytes 7066849 | solution.py:105
  980.1 11.9 convolution_bitcast_fusion.3
  1033.3 39.9 %all-reduce = (f32[4]{0:T(128)S(1)}, f32[]{:T(128)}) all-reduce(f32[4]{0:T(128)S(1)} %pad_maximum_fusion.8, f32[]{:T(128)} %convert_reduce_fusion), channel_id=1, replica_groups=mesh['dp'=8,'frames'=4] {'dp','frames'}, use_global_device_ids=true, to_apply=%region_68.69 | all-reduce | flops 5 | bytes 40 | tf_op jit(solution)/shard_map/psum | solution.py:325
  1074.4 11.7 fusion.148
  1087.3 12.7 reduce-scatter.38.cloned.1.call-done
  1101.4 130.8 %reduce-scatter.36.cloned.1.call-done = f32[32,4]{1,0:T(8,128)} async-done(((f32[1024,4]{1,0:T(8,128)}), f32[32,4]{1,0:T(8,128)}) %reduce-scatter.36.cloned.1.call-update) | async-done | bytes 528
  1233.6 138.3 %reduce-scatter.28.cloned.1.call-done = f32[32,1024]{1,0:T(8,128)} async-done(((f32[1024,1024]{1,0:T(8,128)}), f32[32,1024]{1,0:T(8,128)}) %reduce-scatter.28.cloned.1.call-update) | async-done | bytes 131088 | tf_op jit(solution)/shard_map/reduce_scatter | solution.py:418
  1372.0 139.5 %reduce-scatter.26.cloned.1.call-done = f32[32,1024]{1,0:T(8,128)} async-done(((f32[1024,1024]{1,0:T(8,128)}), f32[32,1024]{1,0:T(8,128)}) %reduce-scatter.26.cloned.1.call-update) | async-done | bytes 131088 | tf_op jit(solution)/shard_map/reduce_scatter | solution.py:416
  1511.4 139.5 %reduce-scatter.24.cloned.1.call-done = f32[32,1024]{1,0:T(8,128)} async-done(((f32[1024,1024]{1,0:T(8,128)}), f32[32,1024]{1,0:T(8,128)}) %reduce-scatter.24.cloned.1.call-update) | async-done | bytes 131088 | tf_op jit(solution)/shard_map/reduce_scatter | solution.py:415
  1651.0 147.5 %reduce-scatter.34.cloned.1.call-done = f32[32,2048]{1,0:T(8,128)} async-done(((f32[1024,2048]{1,0:T(8,128)}), f32[32,2048]{1,0:T(8,128)}) %reduce-scatter.34.cloned.1.call-update) | async-done | bytes 262160
  1798.5 157.8 %reduce-scatter.22.cloned.1.call-done = f32[32,3072]{1,0:T(8,128)} async-done(((f32[1024,3072]{1,0:T(8,128)}), f32[32,3072]{1,0:T(8,128)}) %reduce-scatter.22.cloned.1.call-update) | async-done | bytes 393232 | tf_op jit(solution)/shard_map/reduce_scatter | solution.py:414
  1956.3 184.8 %reduce-scatter.30.cloned.1.call-done = f32[32,4096]{1,0:T(8,128)} async-done(((f32[1024,4096]{1,0:T(8,128)}), f32[32,4096]{1,0:T(8,128)}) %reduce-scatter.30.cloned.1.call-update) | async-done | bytes 524304 | tf_op jit(solution)/shard_map/reduce_scatter | solution.py:419
  2141.1 187.5 %reduce-scatter.32.cloned.1.call-done = f32[128,1024]{1,0:T(8,128)} async-done(((f32[4096,1024]{1,0:T(8,128)}), f32[128,1024]{1,0:T(8,128)}) %reduce-scatter.32.cloned.1.call-update) | async-done | bytes 524304 | tf_op jit(solution)/shard_map/reduce_scatter | solution.py:420
  (865 shorter events, 694.1 us)
Async XLA Ops:
  7.2 255.7 %copy-start = (bf16[4,376,1024]{2,1,0:T(8,128)(2,1)S(1)}, bf16[4,376,1024]{2,1,0:T(8,128)(2,1)}, u32[]{:S(2)}) copy-start(bf16[4,376,1024]{2,1,0:T(8,128)(2,1)} %param.36) | copy-start | bytes 9240580
  7.2 86.9 %all-gather.14.cloned.1.call-start = ((), (), s32[]{:S(2)}) async-start(), calls=%async_computation.11 | async-start | bytes 6488064 | tf_op jit(solution)/shard_map/all_gather | solution.py:223
  7.9 133.2 %all-gather.16.cloned.1.call-start = ((), (), s32[]{:S(2)}) async-start(), calls=%async_computation.12 | async-start | bytes 2162688 | tf_op jit(solution)/shard_map/all_gather | solution.py:224
  8.7 190.6 %all-gather.18.cloned.1.call-start = ((), (), s32[]{:S(2)}) async-start(), calls=%async_computation.13 | async-start | bytes 2162688 | tf_op jit(solution)/shard_map/all_gather | solution.py:225
  9.4 253.5 %all-gather.20.cloned.1.call-start = ((), (), s32[]{:S(2)}) async-start(), calls=%async_computation.14 | async-start | bytes 4325376 | tf_op jit(solution)/shard_map/all_gather | solution.py:226
  10.0 274.7 %all-gather.28.cloned.1.call-start = ((), (), s32[]{:S(2)}) async-start(), calls=%async_computation.26 | async-start | bytes 1310720 | tf_op jit(solution)/shard_map/all_gather | solution.py:268
  94.0 105.3 %copy-start.41 = (f32[1,1024]{1,0:T(1,128)}, f32[1,1024]{1,0:T(1,128)S(1)}, u32[]{:S(2)}) copy-start(f32[1,1024]{1,0:T(1,128)S(1)} %get-tuple-element.1125) | copy-start | bytes 12292
  94.0 517.9 %copy-start.35 = (f32[1,1024]{1,0:T(1,128)}, f32[1,1024]{1,0:T(1,128)S(1)}, u32[]{:S(2)}) copy-start(f32[1,1024]{1,0:T(1,128)S(1)} %get-tuple-element.1124) | copy-start | bytes 12292
  94.1 105.2 %copy-start.43 = (f32[1,1024]{1,0:T(1,128)}, f32[1,1024]{1,0:T(1,128)S(1)}, u32[]{:S(2)}) copy-start(f32[1,1024]{1,0:T(1,128)S(1)} %get-tuple-element.1129) | copy-start | bytes 12292
  94.1 421.5 %copy-start.39 = (f32[1,1024]{1,0:T(1,128)}, f32[1,1024]{1,0:T(1,128)S(1)}, u32[]{:S(2)}) copy-start(f32[1,1024]{1,0:T(1,128)S(1)} %get-tuple-element.1128) | copy-start | bytes 12292
  144.2 127.7 %copy-start.49 = (f32[128]{0:T(128)}, f32[128]{0:T(128)S(1)}, u32[]{:S(2)}) copy-start(f32[128]{0:T(128)S(1)} %broadcast_multiply_fusion.2) | copy-start | bytes 1540
  145.2 126.7 %copy-start.62 = (f32[128]{0:T(128)}, f32[128]{0:T(128)S(1)}, u32[]{:S(2)}) copy-start(f32[128]{0:T(128)S(1)} %multiply_reduce_fusion.11) | copy-start | bytes 1540
  202.3 211.4 %all-gather.22.cloned.1.call-start = ((), (), s32[]{:S(2)}) async-start(), calls=%async_computation.16 | async-start | bytes 2162688 | tf_op jit(solution)/shard_map/all_gather | solution.py:227
  202.9 232.0 %reduce-scatter.18.cloned.1.call-start = ((), (), s32[]{:S(2)}) async-start(), calls=%async_computation.15 | async-start | bytes 1310720 | tf_op jit(solution)/shard_map/reduce_scatter | solution.py:303
  411.0 104.6 %all-gather.24.cloned.1.call-start = ((), (), s32[]{:S(2)}) async-start(), calls=%async_computation.17 | async-start | bytes 8650752 | tf_op jit(solution)/shard_map/all_gather | solution.py:228
  411.8 183.2 %all-gather.26.cloned.1.call-start = ((), (), s32[]{:S(2)}) async-start(), calls=%async_computation.18 | async-start | bytes 8650752 | tf_op jit(solution)/shard_map/all_gather | solution.py:229
  412.5 218.2 %all-gather.30.cloned.1.call-start = ((), (), s32[]{:S(2)}) async-start(), calls=%async_computation.27 | async-start | bytes 1310720 | tf_op jit(solution)/shard_map/all_gather | solution.py:340
  437.9 174.1 %copy-start.47 = (f32[128]{0:T(128)}, f32[128]{0:T(128)S(1)}, u32[]{:S(2)}) copy-start(f32[128]{0:T(128)S(1)} %broadcast_multiply_fusion.1) | copy-start | bytes 1540
  438.9 173.1 %copy-start.53 = (f32[128]{0:T(128)}, f32[128]{0:T(128)S(1)}, u32[]{:S(2)}) copy-start(f32[128]{0:T(128)S(1)} %fusion.180) | copy-start | bytes 1540
  615.3 305.7 %reduce-scatter.20.cloned.1.call-start = ((), (), s32[]{:S(2)}) async-start(), calls=%async_computation.19 | async-start | bytes 1310720 | tf_op jit(solution)/shard_map/reduce_scatter | solution.py:377
  712.7 208.2 %copy-start.42 = (f32[1,1024]{1,0:T(1,128)S(1)}, f32[1,1024]{1,0:T(1,128)}, u32[]{:S(2)}) copy-start(f32[1,1024]{1,0:T(1,128)} %copy-done.41) | copy-start | bytes 12292
  712.7 208.2 %copy-start.50 = (f32[128]{0:T(128)S(1)}, f32[128]{0:T(128)}, u32[]{:S(2)}) copy-start(f32[128]{0:T(128)} %copy-done.49) | copy-start | bytes 1540
  712.7 208.2 %copy-start.56 = (f32[128]{0:T(128)S(1)}, f32[128]{0:T(128)}, u32[]{:S(2)}) copy-start(f32[128]{0:T(128)} %copy-done.55) | copy-start | bytes 1540
  894.9 205.2 %reduce-scatter.38.cloned.1.call-start = ((), (), s32[]{:S(2)}) async-start(), calls=%async_computation.30 | async-start | bytes 540672
  965.6 266.6 %reduce-scatter.36.cloned.1.call-start = ((), (), s32[]{:S(2)}) async-start(), calls=%async_computation.29 | async-start | bytes 540672
  966.8 405.1 %reduce-scatter.28.cloned.1.call-start = ((), (), s32[]{:S(2)}) async-start(), calls=%async_computation.23 | async-start | bytes 4325376 | tf_op jit(solution)/shard_map/reduce_scatter | solution.py:418
  970.6 540.8 %reduce-scatter.26.cloned.1.call-start = ((), (), s32[]{:S(2)}) async-start(), calls=%async_computation.22 | async-start | bytes 4325376 | tf_op jit(solution)/shard_map/reduce_scatter | solution.py:416
  975.4 675.6 %reduce-scatter.24.cloned.1.call-start = ((), (), s32[]{:S(2)}) async-start(), calls=%async_computation.21 | async-start | bytes 4325376 | tf_op jit(solution)/shard_map/reduce_scatter | solution.py:415
  980.0 818.4 %reduce-scatter.34.cloned.1.call-start = ((), (), s32[]{:S(2)}) async-start(), calls=%async_computation.28 | async-start | bytes 8650752
  1001.2 955.1 %reduce-scatter.22.cloned.1.call-start = ((), (), s32[]{:S(2)}) async-start(), calls=%async_computation.20 | async-start | bytes 12976128 | tf_op jit(solution)/shard_map/reduce_scatter | solution.py:414
  1009.8 1131.4 %reduce-scatter.30.cloned.1.call-start = ((), (), s32[]{:S(2)}) async-start(), calls=%async_computation.24 | async-start | bytes 17301504 | tf_op jit(solution)/shard_map/reduce_scatter | solution.py:419
  1020.0 1308.6 %reduce-scatter.32.cloned.1.call-start = ((), (), s32[]{:S(2)}) async-start(), calls=%async_computation.25 | async-start | bytes 17301504 | tf_op jit(solution)/shard_map/reduce_scatter | solution.py:420
  (126 other events, 562.5 us)
Sparse Core Ops, SparseCore 0:
  10.9 72.3 all-gather.13
  86.1 55.0 all-gather.15
  144.0 55.2 all-gather.17
  202.0 60.8 all-gather.19
  264.9 15.2 all-gather.27
  282.9 56.4 all-gather.21
  411.1 23.6 reduce-scatter.17
  438.1 77.4 all-gather.23
  518.9 76.0 all-gather.25
  615.4 15.2 all-gather.29
  895.0 25.9 reduce-scatter.19
  965.8 134.2 reduce-scatter.37
  1102.4 129.8 reduce-scatter.35
  1235.0 136.9 reduce-scatter.27
  1374.7 136.7 reduce-scatter.25
  1514.1 136.7 reduce-scatter.23
  1653.7 144.7 reduce-scatter.33
  1804.9 151.3 reduce-scatter.21
  1959.3 181.8 reduce-scatter.29
  2143.9 184.6 reduce-scatter.31
where the time goes:
time: 2350 us; the launch traced here: 2340 us
  waiting for transfers between devices  1590 us (68%)
  matrix products  350 us (15%)
  local copies, waits for them, and re-layouts  208 us (9%)
  blocking collectives  153 us (7%)
    unnamed x23, waiting for transfers between devices  296 us
    reduce_scatter x1, waiting for transfers between devices, local(): lax.psum_scatter(contract_grad, ('dp', 'frames'), scatter_dimension=0, ti...  187 us
    reduce_scatter x1, waiting for transfers between devices, local(): lax.psum_scatter(expand_grad, ('dp', 'frames'), scatter_dimension=0, tile...  185 us
    reduce_scatter x1, waiting for transfers between devices, local(): lax.psum_scatter(self_project_grad, ('dp', 'frames'), scatter_dimension=0...  158 us
    reduce_scatter x1, waiting for transfers between devices, local(): lax.psum_scatter(self_output_grad, ('dp', 'frames'), scatter_dimension=0,...  140 us
    reduce_scatter x1, waiting for transfers between devices, local(): lax.psum_scatter(cross_query_grad, ('dp', 'frames'), scatter_dimension=0,...  139 us
    reduce_scatter x1, waiting for transfers between devices, local(): lax.psum_scatter(cross_output_grad, ('dp', 'frames'), scatter_dimension=0...  138 us
    dot_general x21, matrix products, matmul(): return jnp.dot(left_side, right_side, preferred_element_type=jnp.float32)  119 us
  transfers between devices with their start and end apart: 20, of which 17 were waited for; matrix products, arithmetic and copies ran while one was open for 11% of the time, Pallas kernels for 0%

commit v1 on v0

--- a/solution.py
+++ b/solution.py
@@ -1,11 +1,511 @@
+import functools
+from types import SimpleNamespace
+
 import jax
 import jax.numpy as jnp
 from jax import lax
+from jax.experimental import pallas as pl
+from jax.experimental.pallas import tpu as pltpu
 from jax.sharding import PartitionSpec as P
 
+MESH = pl.DeviceIdType.MESH
+F32 = jnp.float32
+BF16 = jnp.bfloat16
 HEAD_DIM = 64
-
-
+LANES = 128
+TILE = 256
+
+
+def dot(a, b):
+    return jnp.dot(a, b, preferred_element_type=F32)
+
+
+def dot_nt(a, b):
+    return lax.dot_general(a, b, (((1,), (1,)), ((), ())), preferred_element_type=F32)
+
+
+def place():
+    dp, fr = lax.axis_index("dp"), lax.axis_index("frames")
+    z, y = lax.div(dp, 2), lax.rem(dp, 2)
+    x, c = lax.div(fr, 2), lax.rem(fr, 2)
+
+    def dev(zz, yy, xx, cc):
+        return {"dp": zz * 2 + yy, "frames": xx * 2 + cc}
+
+    me = SimpleNamespace(z=z, y=y, x=x, c=c, fr=fr, dev=dev)
+    me.xn = dev(z, y, 1 - x, c)
+    me.yn = dev(z, 1 - y, x, c)
+    me.sib = dev(z, y, x, 1 - c)
+    me.diag = dev(z, y, 1 - x, 1 - c)
+    me.j = y * 4 + x * 2 + c
+    me.jx = y * 4 + (1 - x) * 2 + c
+    me.jy = (1 - y) * 4 + x * 2 + c
+    me.jxy = (1 - y) * 4 + (1 - x) * 2 + c
+    me.flip = 1 - 2 * c
+    return me
+
+
+def remote(src, dst, send, recv, device):
+    return pltpu.make_async_remote_copy(
+        src_ref=src, dst_ref=dst, send_sem=send, recv_sem=recv, device_id=device, device_id_type=MESH
+    )
+
+
+def gather_steps(me, w, send, recv, nz):
+    half = w.shape[2] // 2
+
+    def cp(view, s, device):
+        return remote(view, view, send.at[s], recv.at[s], device)
+
+    def step_z():
+        for dz in range(1, nz):
+            to = me.dev(lax.rem(me.z + dz, nz), me.y, me.x, me.c)
+            cp(w.at[me.z, me.j], dz - 1, to).start()
+
+    def step_near():
+        for dz in range(1, nz):
+            cp(w.at[lax.rem(me.z + nz - dz, nz), me.j], dz - 1, me.xn).wait_recv()
+        cp(w.at[:, me.j], nz - 1, me.xn).start()
+        cp(w.at[:, me.j], nz, me.yn).start()
+        cp(w.at[:, me.j], nz + 1, me.sib).start()
+
+    def step_far():
+        cp(w.at[:, me.jx], nz - 1, me.xn).wait_recv()
+        cp(w.at[:, me.jx, 0:half], nz + 2, me.yn).start()
+        cp(w.at[:, me.jx], nz + 3, me.sib).start()
+        cp(w.at[:, me.jy], nz, me.yn).wait_recv()
+        cp(w.at[:, me.jy, half:], nz + 4, me.xn).start()
+        cp(w.at[:, me.jy], nz + 5, me.sib).start()
+
+    def step_last():
+        cp(w.at[:, me.jxy, 0:half], nz + 2, me.yn).wait_recv()
+        cp(w.at[:, me.jxy, half:], nz + 4, me.xn).wait_recv()
+        cp(w.at[:, me.jxy], nz + 6, me.sib).start()
+
+    def step_done():
+        for at, s in ((me.j, nz + 1), (me.jx, nz + 3), (me.jy, nz + 5), (me.jxy, nz + 6)):
+            cp(w.at[:, at + me.flip], s, me.sib).wait_recv()
+
+    def drain():
+        for dz in range(1, nz):
+            cp(w.at[me.z, me.j], dz - 1, me.xn).wait_send()
+        for at, s in ((me.j, nz - 1), (me.j, nz), (me.j, nz + 1), (me.jx, nz + 3), (me.jy, nz + 5), (me.jxy, nz + 6)):
+            cp(w.at[:, at], s, me.xn).wait_send()
+        cp(w.at[:, me.jx, 0:half], nz + 2, me.xn).wait_send()
+        cp(w.at[:, me.jy, half:], nz + 4, me.xn).wait_send()
+
+    return SimpleNamespace(z=step_z, near=step_near, far=step_far, last=step_last, done=step_done, drain=drain)
+
+
+def lane_masks():
+    lane = lax.broadcasted_iota(jnp.int32, (1, LANES), 1)
+    left = jnp.where(lane < HEAD_DIM, 1.0, 0.0).astype(BF16)
+    return left, (1.0 - left.astype(F32)).astype(BF16)
+
+
+def two_heads(block):
+    left, right = lane_masks()
+    return jnp.concatenate([block * left, block * right], axis=0)
+
+
+def one_block(pair):
+    rows = pair.shape[0] // 2
+    lane = lax.broadcasted_iota(jnp.int32, (rows, LANES), 1)
+    return jnp.where(lane < HEAD_DIM, pair[:rows], pair[rows:])
+
+
+def at128(p, base=0):
+    return pl.ds(pl.multiple_of(base + p * LANES, LANES), LANES)
+
+
+def put_stat(stat, p, pair):
+    rows = pair.shape[0] // 2
+    lane = lax.broadcasted_iota(jnp.int32, stat.shape, 1)
+    stat = jnp.where(lane == 2 * p, pair[:rows], stat)
+    return jnp.where(lane == 2 * p + 1, pair[rows:], stat)
+
+
+def normalise(values):
+    center = values - jnp.mean(values, axis=-1, keepdims=True)
+    spread = jnp.mean(center * center, axis=-1, keepdims=True)
+    return center * lax.rsqrt(spread + 1e-05)
+
+
+def forward(r, me, nz):
+    d = r.tokens.shape[1]
+    rows = r.tokens.shape[0]
+    items = r.memory.shape[0]
+    frames = r.memory.shape[1]
+    pairs = d // LANES
+
+    def weight(k, n):
+        return r.wg[k, :, :, :, pl.ds(pl.multiple_of(n * TILE, TILE), TILE)].reshape(d, TILE)
+
+    def product(x, k, sink):
+        def body(n, carry):
+            sink(n, pl.ds(pl.multiple_of(n * TILE, TILE), TILE), dot(x, weight(k, n)))
+            return carry
+
+        lax.fori_loop(0, d // TILE, body, 0)
+
+    def ln(values, i):
+        return normalise(values) * r.gs[i : i + 1, :] + r.gs[4 + i : 5 + i, :]
+
+    def norms_in():
+        for g in range(2 * nz):
+            zz, base = g // 2, 4 * (g % 2)
+            total = r.ng[zz, base, 0:16, :].astype(F32)
+            for f in range(1, 4):
+                total = total + r.ng[zz, base + f, 0:16, :].astype(F32)
+            r.gs[:, g * LANES : (g + 1) * LANES] = total
+
+    def norm_one():
+        r.n1[...] = ln(r.tokens[...], 0).astype(BF16)
+        r.n1t[...] = r.n1[...].T
+
+    def joint(q):
+        def sink(n, cols, v):
+            r.joint[:, pl.ds(pl.multiple_of(q * d + n * TILE, TILE), TILE)] = v.astype(BF16)
+
+        product(r.n1[...], q, sink)
+
+    def self_attention():
+        row = lax.rem(lax.broadcasted_iota(jnp.int32, (2 * rows, rows), 0), rows)
+        causal = row >= lax.broadcasted_iota(jnp.int32, (2 * rows, rows), 1)
+
+        def body(p, stat):
+            q2 = two_heads(r.joint[:, at128(p)] * jnp.asarray(HEAD_DIM**-0.5, BF16))
+            s = dot_nt(q2, r.joint[:, at128(p, d)])
+            s = jnp.where(causal, s, -1e30)
+            m = jnp.max(s, axis=-1, keepdims=True)
+            e = jnp.exp(s - m)
+            total = jnp.sum(e, axis=-1, keepdims=True)
+            o2 = dot(e.astype(BF16), r.joint[:, at128(p, 2 * d)]) / total
+            r.smix[:, at128(p)] = one_block(o2).astype(BF16)
+            return put_stat(stat, p, m + jnp.log(total))
+
+        stat = lax.fori_loop(0, pairs, body, jnp.zeros((rows, LANES), F32))
+        r.slse[...] = stat.T
+        r.smixt[...] = r.smix[...].T
+
+    def self_out():
+        def sink(n, cols, v):
+            r.branch[:, cols] = v
+
+        product(r.smix[...], 3, sink)
+        r.first[...] = r.tokens[...] + r.branch[...]
+        squares(1, r.branch[...])
+        r.n2[...] = ln(r.first[...], 1).astype(BF16)
+        r.n2t[...] = r.n2[...].T
+
+    def squares(i, values):
+        ok = lax.broadcasted_iota(jnp.int32, (rows, 1), 0) < r.tl[0]
+        total = jnp.sum(jnp.where(ok, values * values, 0.0))
+        line = lax.broadcasted_iota(jnp.int32, r.sq.shape, 0)
+        r.sq[...] = jnp.where(line == i, total, r.sq[...])
+
+    def start_counts():
+        line = lax.broadcasted_iota(jnp.int32, r.sq.shape, 0)
+        r.sq[...] = jnp.where(line == 4, r.tl[0].astype(F32), 0.0)
+
+    def queries():
+        def sink(n, cols, v):
+            r.qa[me.fr, :, cols] = v.astype(BF16)
+
+        product(r.n2[...], 4, sink)
+
+    def q_copy(f, s, device):
+        return remote(r.qa.at[f], r.qa.at[f], r.q_send.at[s], r.q_recv.at[s], device)
+
+    fx, fs, fd = (1 - me.x) * 2 + me.c, me.x * 2 + 1 - me.c, (1 - me.x) * 2 + 1 - me.c
+
+    def q_start():
+        q_copy(me.fr, 0, me.xn).start()
+        q_copy(me.fr, 1, me.sib).start()
+
+    def q_forward():
+        q_copy(fx, 0, me.xn).wait_recv()
+        q_copy(fx, 2, me.sib).start()
+
+    def q_done():
+        q_copy(fs, 1, me.sib).wait_recv()
+        q_copy(fd, 2, me.sib).wait_recv()
+
+    def mem_copy(t):
+        return pltpu.make_async_copy(r.memory.at[t], r.stage.at[t % 2], r.m_sem.at[t % 2])
+
+    def memory_part(which):
+        def item(t):
+            mem_copy(t).wait()
+
+            def body(n, carry):
+                v = dot(r.stage[t % 2], weight(5 + which, n))
+                r.kv[t, :, pl.ds(pl.multiple_of(which * d + n * TILE, TILE), TILE)] = v.astype(BF16)
+                return carry
+
+            lax.fori_loop(0, d // TILE, body, 0)
+            if which == 0:
+                r.memt[:, t * frames : (t + 1) * frames] = r.stage[t % 2].T
+            if t + 2 < items:
+                mem_copy(t + 2).start()
+
+        def run():
+            for t in range(items):
+                item(t)
+            if which == 0:
+                for t in range(min(2, items)):
+                    mem_copy(t).start()
+
+        return run
+
+    def mem_start():
+        for t in range(min(2, items)):
+            mem_copy(t).start()
+
+    def cross_item(t):
+        def body(p, stat):
+            q2 = two_heads(r.qa[t, :, at128(p)] * jnp.asarray(HEAD_DIM**-0.5, BF16))
+            s = dot_nt(q2, r.kv[t, :, at128(p)]) + r.bias[pl.ds(t, 1), :]
+            m = jnp.max(s, axis=-1, keepdims=True)
+            e = jnp.exp(s - m)
+            total = jnp.sum(e, axis=-1, keepdims=True)
+            o2 = dot(e.astype(BF16), r.kv[t, :, at128(p, d)]) / total
+            r.op[t, :, at128(p)] = one_block(o2).astype(BF16)
+            return put_stat(stat, p, m + jnp.log(total))
+
+        stat = lax.fori_loop(0, pairs, body, jnp.zeros((rows, LANES), F32))
+        r.opl[t] = stat.T
+
+    def o_copies(t, slot, device):
+        return (
+            remote(r.op.at[t], r.orv.at[slot], r.o_send.at[slot], r.o_recv.at[slot], device),
+            remote(r.opl.at[t, 0:16], r.orl.at[slot, 0:16], r.o_send.at[3 + slot], r.o_recv.at[3 + slot], device),
+        )
+
+    def o_start(t, slot, device):
+        for cp in o_copies(t, slot, device):
+            cp.start()
+
+    def o_wait(t, slot, device):
+        for cp in o_copies(t, slot, device):
+            cp.wait_recv()
+
+    def merge(parts, sink):
+        lses = [lse[0:16] for _, lse in parts]
+        top = functools.reduce(jnp.maximum, lses)
+        shares = [jnp.exp(v - top) for v in lses]
+        total = functools.reduce(jnp.add, shares)
+        flat = jnp.concatenate([v / total for v in shares] + [jnp.zeros((LANES - 16 * len(parts), LANES), F32)], axis=0)
+        r.wcol[...] = flat.T
+        lane = lax.broadcasted_iota(jnp.int32, (rows, LANES), 1)
+        for p in range(pairs):
+            value = jnp.zeros((rows, LANES), F32)
+            for i, (mix, _) in enumerate(parts):
+                left = r.wcol[:, 16 * i + 2 * p : 16 * i + 2 * p + 1]
+                right = r.wcol[:, 16 * i + 2 * p + 1 : 16 * i + 2 * p + 2]
+                share = jnp.where(lane < HEAD_DIM, left, right)
+                value = value + share * mix[:, p * LANES : (p + 1) * LANES].astype(F32)
+            sink(p, value)
+        return top + jnp.log(total)
+
+    def cross_a():
+        cross_item(fd)
+        o_start(fd, 0, me.sib)
+        cross_item(fs)
+        o_start(fs, 1, me.sib)
+
+    def cross_b():
+        cross_item(fx)
+        o_wait(fd, 0, me.sib)
+
+        def sink(p, v):
+            r.op[fx, :, p * LANES : (p + 1) * LANES] = v.astype(BF16)
+
+        lse = merge([(r.op.at[fx], r.opl.at[fx]), (r.orv.at[0], r.orl.at[0])], sink)
+        r.opl[fx, 0:16] = lse
+        o_start(fx, 2, me.xn)
+        cross_item(me.fr)
+
+    def cross_c():
+        o_wait(fs, 1, me.sib)
+        o_wait(fx, 2, me.xn)
+
+        def sink(p, v):
+            r.cmix[:, p * LANES : (p + 1) * LANES] = v
+
+        parts = [(r.op.at[me.fr], r.opl.at[me.fr]), (r.orv.at[1], r.orl.at[1]), (r.orv.at[2], r.orl.at[2])]
+        r.clse[0:16] = merge(parts, sink)
+        r.cmixt[...] = r.cmix[...].T.astype(BF16)
+
+    def cross_out():
+        def sink(n, cols, v):
+            r.branch[:, cols] = v
+
+        product(r.cmix[...].astype(BF16), 7, sink)
+        squares(2, r.branch[...])
+        r.second[...] = r.first[...] + r.branch[...]
+        r.n3[...] = ln(r.second[...], 2).astype(BF16)
+        r.n3t[...] = r.n3[...].T
+
+    def expand(q):
+        def sink(n, cols, v):
+            at = pl.ds(pl.multiple_of(q * d + n * TILE, TILE), TILE)
+            half = 0.5 * (1.0 + lax.erf(v * (2.0**-0.5)))
+            r.active[:, at] = (v * half).astype(BF16)
+            r.slope[:, at] = (half + v * jnp.exp(-0.5 * v * v) * 0.3989422804014327).astype(BF16)
+
+        product(r.n3[...], 8 + q, sink)
+        r.activet[q * d : (q + 1) * d, :] = r.active[:, q * d : (q + 1) * d].T
+
+    def contract(q):
+        def sink(n, cols, v):
+            r.branch[:, cols] = v if q == 0 else r.branch[:, cols] + v
+
+        product(r.active[:, q * d : (q + 1) * d], 12 + q, sink)
+
+    def finish():
+        squares(3, r.branch[...])
+        r.third[...] = r.second[...] + r.branch[...]
+        squares(0, r.third[...])
+        ok = lax.broadcasted_iota(jnp.int32, (rows, 1), 0) < r.tl[0]
+        r.result[...] = jnp.where(ok, ln(r.third[...], 3), 0.0)
+
+    def at(k):
+        return k + 3
+
+    tasks = {}
+
+    def add(tick, *fs):
+        tasks.setdefault(tick, []).extend(fs)
+
+    add(0, start_counts, mem_start)
+    add(2, norms_in, norm_one)
+    for q in range(3):
+        add(at(q), functools.partial(joint, q))
+    add(at(2), self_attention)
+    add(at(3), self_out)
+    add(at(4), queries, q_start)
+    add(at(5), q_forward, memory_part(0))
+    add(at(6), memory_part(1), q_done, cross_a)
+    add(at(7), cross_b)
+    add(at(8), cross_c, cross_out)
+    for q in range(4):
+        add(at(8 + q), functools.partial(expand, q))
+        add(at(12 + q), functools.partial(contract, q))
+    add(at(15), finish)
+
+    def drain():
+        q_copy(me.fr, 0, me.xn).wait_send()
+        q_copy(me.fr, 1, me.sib).wait_send()
+        q_copy(fx, 2, me.sib).wait_send()
+        for t, slot, device in ((fd, 0, me.sib), (fs, 1, me.sib), (fx, 2, me.xn)):
+            for cp in o_copies(t, slot, device):
+                cp.wait_send()
+
+    return tasks, drain
+
+
+def run_forward(r, me, nz, chunks):
+    own = pltpu.make_async_copy(r.shards, r.wg.at[:, me.z, me.j], r.own_sem.at[0])
+    own.start()
+    r.ng[me.z, me.j] = r.norms[...]
+    barrier = pltpu.get_barrier_semaphore()
+    peers = [me.xn, me.yn, me.sib, me.diag]
+    peers += [me.dev(lax.rem(me.z + dz, nz), me.y, me.x, me.c) for dz in range(1, nz)]
+    for device in peers:
+        pl.semaphore_signal(barrier, inc=1, device_id=device, device_id_type=MESH)
+    pl.semaphore_wait(barrier, len(peers))
+    norm = gather_steps(me, r.ng, r.g_send.at[chunks], r.g_recv.at[chunks], nz)
+    steps = [gather_steps(me, r.wg.at[k], r.g_send.at[k], r.g_recv.at[k], nz) for k in range(chunks)]
+    norm.z()
+    own.wait()
+    steps[0].z()
+    steps[1].z()
+    norm.near()
+    norm.far()
+    norm.last()
+    tasks, drain = forward(r, me, nz)
+    for tick in range(chunks + 3):
+        if tick + 2 < chunks:
+            steps[tick + 2].z()
+        if tick < chunks:
+            steps[tick].near()
+        if 0 <= tick - 1 < chunks:
+            steps[tick - 1].far()
+        if 0 <= tick - 2 < chunks:
+            steps[tick - 2].last()
+        if 0 <= tick - 3 < chunks:
+            steps[tick - 3].done()
+        if tick == 1:
+            norm.done()
+        for task in tasks.get(tick, ()):
+            task()
+    drain()
+    norm.drain()
+    for s in steps:
+        s.drain()
+CHUNKS = 16
+def f_call(nz, tl, tokens, mem_pad, shards, norms, bias):
+    rows, d = tokens.shape
+    items, frames, _ = mem_pad.shape
+    outs = dict(
+        result=((rows, d), F32), wg=((CHUNKS, nz, 8, 32, d), BF16), gs=((16, d), F32),
+        n1t=((d, rows), BF16), joint=((rows, 3 * d), BF16), smixt=((d, rows), BF16), slse=((LANES, LANES), F32),
+        first=((rows, d), F32), n2t=((d, rows), BF16), qa=((items, rows, d), BF16), kv=((items, frames, 2 * d), BF16),
+        memt=((d, items * frames), BF16), cmix=((rows, d), F32), clse=((LANES, LANES), F32), second=((rows, d), F32), n3t=((d, rows), BF16),
+        activet=((4 * d, rows), BF16), slope=((rows, 4 * d), BF16), third=((rows, d), F32), sq=((8, LANES), F32),
+    )
+    scratch = dict(
+        ng=pltpu.VMEM((nz, 8, 32, LANES), BF16), n1=pltpu.VMEM((rows, d), BF16), smix=pltpu.VMEM((rows, d), BF16),
+        branch=pltpu.VMEM((rows, d), F32), n2=pltpu.VMEM((rows, d), BF16), stage=pltpu.VMEM((2, frames, d), BF16),
+        op=pltpu.VMEM((items, rows, d), BF16), opl=pltpu.VMEM((items, LANES, LANES), F32), orv=pltpu.VMEM((3, rows, d), BF16),
+        orl=pltpu.VMEM((3, LANES, LANES), F32), wcol=pltpu.VMEM((LANES, LANES), F32), cmixt=pltpu.VMEM((d, rows), BF16),
+        n3=pltpu.VMEM((rows, d), BF16), active=pltpu.VMEM((rows, 4 * d), BF16),
+        own_sem=pltpu.SemaphoreType.DMA((1,)), m_sem=pltpu.SemaphoreType.DMA((2,)),
+        g_send=pltpu.SemaphoreType.DMA((CHUNKS + 1, nz + 7)), g_recv=pltpu.SemaphoreType.DMA((CHUNKS + 1, nz + 7)),
+        q_send=pltpu.SemaphoreType.DMA((3,)), q_recv=pltpu.SemaphoreType.DMA((3,)),
+        o_send=pltpu.SemaphoreType.DMA((6,)), o_recv=pltpu.SemaphoreType.DMA((6,)),
+    )
+    ins = ["tl", "tokens", "memory", "shards", "norms", "bias"]
+    names = ins + list(outs) + list(scratch)
+
+    def kernel(*refs):
+        r = SimpleNamespace(**dict(zip(names, refs)))
+        run_forward(r, place(), nz, CHUNKS)
+
+    vm = pl.BlockSpec(memory_space=pltpu.VMEM)
+    res = pl.pallas_call(
+        kernel,
+        out_shape=[jax.ShapeDtypeStruct(s, t) for s, t in outs.values()],
+        in_specs=[pl.BlockSpec(memory_space=pltpu.SMEM), vm, pl.BlockSpec(memory_space=pl.ANY), pl.BlockSpec(memory_space=pl.ANY), vm, vm],
+        out_specs=[vm] * len(outs),
+        scratch_shapes=list(scratch.values()),
+        compiler_params=pltpu.CompilerParams(collective_id=0, has_side_effects=True, vmem_limit_bytes=63 * 2**20),
+    )(tl, tokens, mem_pad, shards, norms, bias)
+    return dict(zip(outs, res))
+
+def pack_weights(ws):
+    self_project, self_output, cross_query, cross_memory, cross_output, expand, contract = ws
+    rows, d = self_output.shape
+    ndev = d // rows
+    cut = lambda w: jnp.transpose(w.reshape(rows, -1, d), (1, 0, 2))
+    q = contract.shape[0] // rows
+    ex = jnp.transpose(expand.reshape(rows, ndev, q, rows), (2, 0, 1, 3)).reshape(q, rows, d)
+    return jnp.concatenate([cut(self_project), cut(self_output), cut(cross_query), cut(cross_memory), cut(cross_output), ex, contract.reshape(q, rows, d)], axis=0)
+
+def pack_norms(gains, shifts):
+    own = jnp.concatenate([gains, shifts], axis=0)
+    lane = (lax.axis_index("frames")) * own.shape[1]
+    return lax.dynamic_update_slice(jnp.zeros((32, LANES), BF16), own, (0, lane))
+
+def frame_bias(cross_mask, memory_length, frame_count, padded):
+    start = lax.axis_index("frames") * frame_count
+    at = start + jnp.arange(frame_count)
+    mask = lax.dynamic_slice_in_dim(cross_mask, start, frame_count, 1)
+    ok = (at[None] < memory_length[:, None]) & ((mask == 1) | (at[None] == 0))
+    return jnp.pad(jnp.where(ok, 0.0, -1e30), ((0, 0), (0, padded - frame_count)), constant_values=-1e30).astype(F32)
+
+NZ = 4
 block_heads = 4
 
 
@@ -200,6 +700,184 @@
         ),
     )
     return (from_blocks(query_grad), from_blocks(key_grad), from_blocks(value_grad))
+
+
+def unmix(part, q):
+    rows, ff = part.shape
+    return jnp.transpose(part.reshape(rows, q, ff // (q * rows), rows), (0, 2, 1, 3)).reshape(rows, ff)
+
+
+def natural(grad, q, rows):
+    ff, d = grad.shape
+    return jnp.transpose(grad.reshape(q, ff // (q * rows), rows, d), (1, 0, 2, 3)).reshape(ff, d)
+
+
+def ln_back(values, gain_row, shift_row, grad):
+    return jax.vjp(layer_norm, values, gain_row, shift_row)[1](grad)
+
+
+def local_fast(
+    tokens,
+    memory,
+    cotangent,
+    self_project,
+    self_output,
+    cross_query,
+    cross_memory,
+    cross_output,
+    expand,
+    contract,
+    norm_gains,
+    norm_shifts,
+    target_length,
+    memory_length,
+    cross_mask,
+):
+    residual_in = tokens[0]
+    length, model_width = residual_in.shape
+    row_valid = jnp.arange(length) < target_length[0]
+    causal = jnp.arange(length)[:, None] >= jnp.arange(length)[None, :]
+    item_count, frame_count = memory.shape[:2]
+    padded = -(-frame_count // LANES) * LANES
+    weights = (self_project, self_output, cross_query, cross_memory, cross_output, expand, contract)
+    bias = frame_bias(cross_mask, memory_length, frame_count, padded)
+    o = f_call(NZ, target_length, residual_in, jnp.pad(memory, ((0, 0), (0, padded - frame_count), (0, 0))), pack_weights(weights), pack_norms(norm_gains, norm_shifts), bias)
+    wg = o["wg"].reshape(CHUNKS, model_width, model_width)
+    join = lambda lo, hi: jnp.concatenate([wg[k] for k in range(lo, hi)], axis=1)
+    w_self, w_self_out, w_query, w_memory, w_cross_out, w_expand = join(0, 3), wg[3], wg[4], join(5, 7), wg[7], join(8, 12)
+    w_contract = jnp.concatenate([wg[k] for k in range(12, 16)], axis=0)
+    gains, shifts = o["gs"][:4], o["gs"][4:8]
+    normed_one, self_mix_low, normed_two, cross_mix_low, normed_three = (
+        o["n1t"].T, o["smixt"].T, o["n2t"].T, o["cmix"].astype(BF16), o["n3t"].T)
+    first_sum, second_sum, third_sum, cross_mix, active, slope = o["first"], o["second"], o["third"], o["cmix"], o["activet"].T, o["slope"].astype(F32)
+    joint_rows = o["joint"]
+    self_queries, self_keys, self_values = (split_heads(joint_rows[:, k * model_width : (k + 1) * model_width]) for k in range(3))
+    heads = model_width // HEAD_DIM
+    self_max = o["slse"][:heads].reshape(-1, block_heads, length)
+    self_totals = jnp.ones_like(self_max)
+    query_heads = split_heads(o["qa"])
+    kv = o["kv"][:, :frame_count]
+    memory_keys, memory_values = split_heads(kv[..., :model_width]), split_heads(kv[..., model_width:])
+    cross_max = lax.all_gather(o["clse"][None, :heads], "frames", axis=0, tiled=True).reshape(item_count, -1, block_heads, length)
+    cross_totals = jnp.ones_like(cross_max)
+    frame_ok = bias[:, :frame_count] == 0.0
+    result = o["result"]
+    total = lax.psum(o["sq"][:5, 0], ("dp", "frames"))
+    squares_all, counted = total[:4], total[4]
+    branch_rms = jnp.sqrt(squares_all / (counted * model_width))
+    grad_result = jnp.where(row_valid[:, None], cotangent[0], 0.0)
+    grad_third, gain_grad_three, shift_grad_three = ln_back(third_sum, gains[3], shifts[3], grad_result)
+    feed_low = grad_third.astype(jnp.bfloat16)
+    contract_grad = matmul(active.T, feed_low)
+    grad_active = matmul(feed_low, w_contract.T)
+    grad_hidden = (grad_active * slope).astype(jnp.bfloat16)
+    expand_grad = matmul(normed_three.T, grad_hidden)
+    grad_normed_three = matmul(grad_hidden, w_expand.T)
+    grad_second_part, gain_grad_two, shift_grad_two = ln_back(second_sum, gains[2], shifts[2], grad_normed_three)
+    grad_second = grad_third + grad_second_part
+    cross_low = grad_second.astype(jnp.bfloat16)
+    cross_output_grad = matmul(cross_mix_low.T, cross_low)
+    grad_cross_mix = matmul(cross_low, w_cross_out.T).astype(jnp.bfloat16)
+    every_grad = split_heads(lax.all_gather(grad_cross_mix[None], "frames", axis=0, tiled=True))
+
+    own_dot = jnp.sum((grad_cross_mix.astype(jnp.float32) * cross_mix).reshape(length, -1, HEAD_DIM), axis=-1).T
+    row_dot = lax.all_gather(own_dot[None], "frames", axis=0, tiled=True).reshape(item_count, -1, block_heads, length)
+
+    def item_grads(inputs):
+        query_item, key_item, value_item, frame_item, grad_item, max_item, total_item, dot_item = (
+            inputs
+        )
+        allowed = jnp.broadcast_to(frame_item[None, :], (length, frame_count))
+        return cross_partial_grads(
+            query_item, key_item, value_item, allowed, grad_item, max_item, total_item, dot_item
+        )
+
+    query_parts, key_parts, value_parts = lax.map(
+        item_grads,
+        (
+            query_heads,
+            memory_keys,
+            memory_values,
+            frame_ok,
+            every_grad,
+            cross_max,
+            cross_totals,
+            row_dot,
+        ),
+    )
+    query_grad = lax.psum_scatter(
+        query_parts.astype(jnp.bfloat16), "frames", scatter_dimension=0, tiled=True
+    ).astype(jnp.float32)[0]
+    memory_low = (
+        jnp.concatenate([key_parts, value_parts], axis=2)
+        .astype(jnp.bfloat16)
+        .reshape(item_count * frame_count, 2 * model_width)
+    )
+    cross_memory_grad = matmul(memory.reshape(item_count * frame_count, model_width).T, memory_low)
+    memory_grad = matmul(memory_low, w_memory.T).reshape(item_count, frame_count, model_width)
+    query_low = query_grad.astype(jnp.bfloat16)
+    cross_query_grad = matmul(normed_two.T, query_low)
+    grad_normed_two = matmul(query_low, w_query.T)
+    grad_first_part, gain_grad_one, shift_grad_one = ln_back(first_sum, gains[1], shifts[1], grad_normed_two)
+    grad_first = grad_second + grad_first_part
+    self_low = grad_first.astype(jnp.bfloat16)
+    self_output_grad = matmul(self_mix_low.T, self_low)
+    grad_self_mix = matmul(self_low, w_self_out.T).astype(jnp.bfloat16)
+    self_query_grad, self_key_grad, self_value_grad = attend_whole_back(
+        self_queries,
+        self_keys,
+        self_values,
+        causal,
+        split_heads(grad_self_mix),
+        self_max,
+        self_totals,
+    )
+    joint_grad = jnp.concatenate([self_query_grad, self_key_grad, self_value_grad], axis=1).astype(
+        jnp.bfloat16
+    )
+    self_project_grad = matmul(normed_one.T, joint_grad)
+    grad_normed_one = matmul(joint_grad, w_self.T)
+    grad_input_part, gain_grad_zero, shift_grad_zero = ln_back(residual_in, gains[0], shifts[0], grad_normed_one)
+    tokens_grad = grad_first + grad_input_part
+    gain_grads = jnp.stack([gain_grad_zero, gain_grad_one, gain_grad_two, gain_grad_three])
+    shift_grads = jnp.stack([shift_grad_zero, shift_grad_one, shift_grad_two, shift_grad_three])
+    reduced = (
+        lax.psum_scatter(self_project_grad, ("dp", "frames"), scatter_dimension=0, tiled=True),
+        lax.psum_scatter(self_output_grad, ("dp", "frames"), scatter_dimension=0, tiled=True),
+        lax.psum_scatter(cross_query_grad, ("dp", "frames"), scatter_dimension=0, tiled=True),
+        lax.psum_scatter(cross_memory_grad, ("dp", "frames"), scatter_dimension=0, tiled=True),
+        lax.psum_scatter(cross_output_grad, ("dp", "frames"), scatter_dimension=0, tiled=True),
+        lax.psum_scatter(expand_grad, ("dp", "frames"), scatter_dimension=0, tiled=True),
+        lax.psum_scatter(natural(contract_grad, contract.shape[0] // expand.shape[0], expand.shape[0]), ("dp", "frames"), scatter_dimension=0, tiled=True),
+        lax.psum_scatter(gain_grads, ("dp", "frames"), scatter_dimension=1, tiled=True),
+        lax.psum_scatter(shift_grads, ("dp", "frames"), scatter_dimension=1, tiled=True),
+    )
+    (
+        project_part,
+        output_part,
+        query_part,
+        memory_part,
+        cross_out_part,
+        expand_part,
+        contract_part,
+        gains_part,
+        shifts_part,
+    ) = reduced
+    return (
+        result[None],
+        tokens_grad[None],
+        memory_grad,
+        project_part,
+        output_part,
+        query_part,
+        memory_part,
+        cross_out_part,
+        unmix(expand_part, contract.shape[0] // expand.shape[0]),
+        contract_part,
+        gains_part,
+        shifts_part,
+        branch_rms,
+    )
 
 
 def local(
@@ -451,7 +1129,7 @@
 
 def solution(mesh):
     return jax.shard_map(
-        local,
+        local_fast if (mesh.shape['dp'], mesh.shape['frames']) == (2 * NZ, 4) else local,
         mesh=mesh,
         in_specs=(
             P(("dp", "frames"), None, None),

time: 2350 us -> 1790 us (0.76)
  waiting for transfers between devices: 1590 us -> 1250 us
  matrix products: 350 us -> 116 us
  Pallas kernels: 0 us -> 192 us
  blocking collectives: 153 us -> 50.7 us
  local copies, waits for them, and re-layouts: 208 us -> 146 us
    all_gather x9 -> x1, waiting for transfers between devices: 298 us -> 0.01 us  [local_fast(): lax.all_gather(grad_cross_mix[None], 'frames', axis=0, tiled=True)]
    pallas_call x0 -> x1, Pallas kernels: none -> 192 us  [f_call(): pl.pallas_call(kernel, out_shape=[jax.ShapeDtypeStruct(s, t) for s, t in...]
    all_gather x2, blocking collectives: 80.8 us -> 11 us  [the longest x1 5.84 us: local_fast(): lax.all_gather(o['clse'][None, :heads], 'frames', axis=0, tiled=True)]
    dot_general x56 -> x20, matrix products: 76.1 us -> 7.86 us  [block_scores(): jnp.einsum('shd,fhd->hsf', query_block, key_block, preferred_element_type...]
    dynamic_slice x48 -> x12, local copies, waits for them, and re-layouts: 63.4 us -> 10.6 us  [local_fast(): lax.map(item_grads, (query_heads, memory_keys, memory_values, frame_ok, e...]
    dot_general x21 -> x14, matrix products: 119 us -> 68.8 us  [matmul(): return jnp.dot(left_side, right_side, preferred_element_type=jnp.float32)]
    dot_general x20 -> x0, matrix products: 43 us -> none  [the longest x16 36.4 us: one_group(): jnp.einsum('hsf,fhd->shd', probs.astype(jnp.bfloat16), value_block, prefe...]
    reduce_scatter x8 -> x7, waiting for transfers between devices: 995 us -> 956 us  [the longest x1 185 us: local_fast(): lax.psum_scatter(natural(contract_grad, contract.shape[0] // expand.shape...]
  transfers between devices with their start and end apart: 20 -> 11, of which waited for: 17 -> 10; matrix products, arithmetic and copies ran while one was open for 11% -> 6% of each run, Pallas kernels for 0% -> 0%
where the time goes in v1:
time: 1790 us
  waiting for transfers between devices  1250 us (70%)
  Pallas kernels  192 us (11%)
  local copies, waits for them, and re-layouts  146 us (8%)
  matrix products  116 us (6%)
  blocking collectives  50.7 us (3%)
    unnamed x14, waiting for transfers between devices  298 us
    pallas_call x1, Pallas kernels, f_call(): pl.pallas_call(kernel, out_shape=[jax.ShapeDtypeStruct(s, t) for s, t in...  192 us
    reduce_scatter x1, waiting for transfers between devices, local_fast(): lax.psum_scatter(natural(contract_grad, contract.shape[0] // expand.shape...  185 us
    reduce_scatter x1, waiting for transfers between devices, local_fast(): lax.psum_scatter(expand_grad, ('dp', 'frames'), scatter_dimension=0, tile...  180 us
    reduce_scatter x1, waiting for transfers between devices, local_fast(): lax.psum_scatter(self_project_grad, ('dp', 'frames'), scatter_dimension=0...  159 us
    reduce_scatter x1, waiting for transfers between devices, local_fast(): lax.psum_scatter(cross_query_grad, ('dp', 'frames'), scatter_dimension=0,...  140 us
    reduce_scatter x1, waiting for transfers between devices, local_fast(): lax.psum_scatter(self_output_grad, ('dp', 'frames'), scatter_dimension=0,...  140 us
    reduce_scatter x1, waiting for transfers between devices, local_fast(): lax.psum_scatter(cross_output_grad, ('dp', 'frames'), scatter_dimension=0...  136 us
  transfers between devices with their start and end apart: 11, of which 10 were waited for; matrix products, arithmetic and copies ran while one was open for 6% of the time, Pallas kernels for 0%

profile of v1, /device:TPU:0, one launch (start us, length us, event | category | flops | bytes accessed | tf_op | source)
XLA Modules:
  0.0 1786.3 jit_solution(13986520128727327097)
XLA Ops:
  23.3 192.4 %shard_map.246 = (f32[128,1024]{1,0:T(8,128)}, bf16[16,4,8,32,1024]{4,3,2,1,0:T(8,128)(2,1)}, f32[16,1024]{1,0:T(8,128)}, bf16[1024,128]{1,0:T(8,128)(2,1)}, bf1...) custom-call(s32[1]{0:T(128)} %copy.192.refs_0_, ...), custom_call_target="tpu_custom_call" | custom-call | tf_op jit(solution)/shard_map/pallas_call | solution.py:477
  219.1 22.1 %fusion.133 = (bf16[1,4,8,32,1024]{4,3,2,1,0:T(8,128)(2,1)}, bf16[1,4,8,32,1024]{4,3,2,1,0:T(8,128)(2,1)}, bf16[1,4,8,32,1024]{4,3,2,1,0:T(8,128)(2,1)}, bf16[1,...) fusion(bf16[16,4,8,32,1024]{4,3,2,1,0:T(8,128)(2,1)} %get-tuple, ...), kind=kLoop, calls=%fused_computation.214 | loop fusion | bytes 67108864 | tf_op jit(solution)/shard_map/slice | solution.py:746
  243.3 6.8 fusion.93
  257.5 5.5 fusion.134
  263.0 4.6 copy.73
  272.4 5.8 all-gather.1
  278.3 5.2 all-gather.2
  289.1 79.4 %while.47 = (s32[]{:T(128)}, bf16[4,128,1024]{1,2,0:T(8,128)(2,1)}, bf16[4,376,1024]{2,1,0:T(8,128)(2,1)}, bf16[4,376,1024]{2,1,0:T(8,128)(2,1)}, bf16[4,128,16,...) while((s32[]{:T(128)}, bf16[4,128,1024]{1,2,0:T(8,128)(2,1)}, ...), condition=%wide.region_12.13_spmd, body=%wide.region_9.12_spmd.sunk | while | flops 124876800 | bytes 25340628 | solution.py:795
  291.8 12.9 while.49
  311.7 12.9 while.49
  331.5 12.9 while.49
  351.3 12.9 while.49
  376.9 17.1 reduce-scatter.17.cloned.1.call-done
  397.6 10.8 while.48
  408.4 6.0 multiply_reduce_fusion.4
  416.7 8.1 fusion.137
  436.0 12.3 convolution_bitcast_fusion.2
  448.3 9.2 copy.92
  458.5 6.4 fusion.100
  468.7 6.8 copy.85
  476.2 39.7 %psum.7 = f32[5]{0:T(128)S(1)} all-reduce(f32[5]{0:T(128)S(1)} %slice_reduce_fusion), channel_id=1, replica_groups=mesh['dp'=8,'frames'=4] {'dp','frames'}, use_global_device_ids=true, to_apply=%region_42.43 | all-reduce | flops 5 | bytes 40 | tf_op jit(solution)/shard_map/psum | solution.py:765
  517.7 11.0 fusion.96
  529.9 19.6 %reduce-scatter.33.cloned.1.call-done = f32[32,4]{1,0:T(8,128)} async-done(((f32[1024,4]{1,0:T(8,128)}), f32[32,4]{1,0:T(8,128)}) %reduce-scatter.33.cloned.1.call-update) | async-done | bytes 528
  550.8 130.7 %reduce-scatter.35.cloned.1.call-done = f32[32,4]{1,0:T(8,128)} async-done(((f32[1024,4]{1,0:T(8,128)}), f32[32,4]{1,0:T(8,128)}) %reduce-scatter.35.cloned.1.call-update) | async-done | bytes 528
  682.9 179.7 %reduce-scatter.27.cloned.1.call-done = f32[32,4096]{1,0:T(8,128)} async-done(((f32[1024,4096]{1,0:T(8,128)}), f32[32,4096]{1,0:T(8,128)}) %reduce-scatter.27.cloned.1.call-update) | async-done | bytes 524304 | tf_op jit(solution)/shard_map/reduce_scatter | solution.py:850
  867.5 4.4 reshape.335
  871.9 135.9 %reduce-scatter.25.cloned.1.call-done = f32[32,1024]{1,0:T(8,128)} async-done(((f32[1024,1024]{1,0:T(8,128)}), f32[32,1024]{1,0:T(8,128)}) %reduce-scatter.25.cloned.1.call-update) | async-done | bytes 131088 | tf_op jit(solution)/shard_map/reduce_scatter | solution.py:849
  1007.9 139.7 %reduce-scatter.21.cloned.1.call-done = f32[32,1024]{1,0:T(8,128)} async-done(((f32[1024,1024]{1,0:T(8,128)}), f32[32,1024]{1,0:T(8,128)}) %reduce-scatter.21.cloned.1.call-update) | async-done | bytes 131088 | tf_op jit(solution)/shard_map/reduce_scatter | solution.py:846
  1147.6 139.8 %reduce-scatter.23.cloned.1.call-done = f32[32,1024]{1,0:T(8,128)} async-done(((f32[1024,1024]{1,0:T(8,128)}), f32[32,1024]{1,0:T(8,128)}) %reduce-scatter.23.cloned.1.call-update) | async-done | bytes 131088 | tf_op jit(solution)/shard_map/reduce_scatter | solution.py:847
  1287.4 147.7 %reduce-scatter.31.cloned.1.call-done = f32[32,2048]{1,0:T(8,128)} async-done(((f32[1024,2048]{1,0:T(8,128)}), f32[32,2048]{1,0:T(8,128)}) %reduce-scatter.31.cloned.1.call-update) | async-done | bytes 262160
  1435.1 158.8 %reduce-scatter.19.cloned.1.call-done = f32[32,3072]{1,0:T(8,128)} async-done(((f32[1024,3072]{1,0:T(8,128)}), f32[32,3072]{1,0:T(8,128)}) %reduce-scatter.19.cloned.1.call-update) | async-done | bytes 393232 | tf_op jit(solution)/shard_map/reduce_scatter | solution.py:845
  1593.9 184.7 %reduce-scatter.29.cloned.1.call-done = f32[128,1024]{1,0:T(8,128)} async-done(((f32[4096,1024]{1,0:T(8,128)}), f32[128,1024]{1,0:T(8,128)}) %reduce-scatter.29.cloned.1.call-update) | async-done | bytes 524304 | tf_op jit(solution)/shard_map/reduce_scatter | solution.py:851
  (452 shorter events, 168.8 us)
Async XLA Ops:
  7.2 276.3 %all-gather.5.cloned.1.call-start = ((), (), s32[]{:S(2)}) async-start(), calls=%async_computation.17 | async-start | bytes 1310720 | tf_op jit(solution)/shard_map/all_gather | solution.py:781
  12.6 7.4 copy-start.33
  12.6 8.1 copy-start.44
  12.6 8.1 copy-start.45
  12.6 8.1 copy-start.46
  219.1 22.1 %copy-start.7 = (f32[128,1024]{1,0:T(8,128)S(1)}, f32[128,1024]{1,0:T(8,128)}, u32[]{:S(2)}) copy-start(f32[128,1024]{1,0:T(8,128)} %get-tuple-element.247) | copy-start | bytes 1572868
  219.1 22.5 %copy-start.22 = (f32[1,128,1024]{2,1,0:T(8,128)S(1)}, f32[1,128,1024]{2,1,0:T(8,128)}, u32[]{:S(2)}) copy-start(f32[1,128,1024]{2,1,0:T(8,128)} %param.23) | copy-start | bytes 1572868
  242.2 11.4 copy-start.10
  243.3 6.9 copy-start.12
  243.3 6.9 copy-start.15
  243.3 6.9 copy-start.16
  243.3 6.9 copy-start.17
  243.3 6.9 copy-start.18
  256.1 137.9 %reduce-scatter.17.cloned.1.call-start = ((), (), s32[]{:S(2)}) async-start(), calls=%async_computation.10 | async-start | bytes 1310720 | tf_op jit(solution)/shard_map/reduce_scatter | solution.py:808
  289.1 80.8 %copy-start.8 = (f32[128,1024]{1,0:T(8,128)S(1)}, f32[128,1024]{1,0:T(8,128)}, u32[]{:S(2)}) copy-start(f32[128,1024]{1,0:T(8,128)} %get-tuple-element.256) | copy-start | bytes 1572868
  368.5 25.5 %copy-start.4 = (bf16[1,4,8,32,1024]{4,3,2,1,0:T(8,128)(2,1)S(1)}, bf16[1,4,8,32,1024]{4,3,2,1,0:T(8,128)(2,1)}, u32[]{:S(2)}) copy-start(bf16[1,4,8,32,1024]{4,3,2,1,0:T(8,128)(2,1)} %get-tuple-element.511) | copy-start | bytes 6291460
  368.5 181.0 %reduce-scatter.33.cloned.1.call-start = ((), (), s32[]{:S(2)}) async-start(), calls=%async_computation.19 | async-start | bytes 540672
  375.4 21.0 %copy-start.6 = (f32[128,1024]{1,0:T(8,128)S(1)}, f32[128,1024]{1,0:T(8,128)}, u32[]{:S(2)}) copy-start(f32[128,1024]{1,0:T(8,128)} %copy-done.5) | copy-start | bytes 1572868
  397.6 10.8 copy-start.9
  408.4 8.3 copy-start.25
  408.4 8.3 copy-start.30
  415.5 266.0 %reduce-scatter.35.cloned.1.call-start = ((), (), s32[]{:S(2)}) async-start(), calls=%async_computation.20 | async-start | bytes 540672
  416.7 446.0 %reduce-scatter.27.cloned.1.call-start = ((), (), s32[]{:S(2)}) async-start(), calls=%async_computation.15 | async-start | bytes 17301504 | tf_op jit(solution)/shard_map/reduce_scatter | solution.py:850
  424.8 583.0 %reduce-scatter.25.cloned.1.call-start = ((), (), s32[]{:S(2)}) async-start(), calls=%async_computation.14 | async-start | bytes 4325376 | tf_op jit(solution)/shard_map/reduce_scatter | solution.py:849
  428.6 719.0 %reduce-scatter.21.cloned.1.call-start = ((), (), s32[]{:S(2)}) async-start(), calls=%async_computation.12 | async-start | bytes 4325376 | tf_op jit(solution)/shard_map/reduce_scatter | solution.py:846
  432.2 855.2 %reduce-scatter.23.cloned.1.call-start = ((), (), s32[]{:S(2)}) async-start(), calls=%async_computation.13 | async-start | bytes 4325376 | tf_op jit(solution)/shard_map/reduce_scatter | solution.py:847
  435.9 999.2 %reduce-scatter.31.cloned.1.call-start = ((), (), s32[]{:S(2)}) async-start(), calls=%async_computation.18 | async-start | bytes 8650752
  457.5 1136.5 %reduce-scatter.19.cloned.1.call-start = ((), (), s32[]{:S(2)}) async-start(), calls=%async_computation.11 | async-start | bytes 12976128 | tf_op jit(solution)/shard_map/reduce_scatter | solution.py:845
  464.9 1313.8 %reduce-scatter.29.cloned.1.call-start = ((), (), s32[]{:S(2)}) async-start(), calls=%async_computation.16 | async-start | bytes 17301504 | tf_op jit(solution)/shard_map/reduce_scatter | solution.py:851
  475.4 42.3 %copy-start.14 = (bf16[1,4,8,32,1024]{4,3,2,1,0:T(8,128)(2,1)S(1)}, bf16[1,4,8,32,1024]{4,3,2,1,0:T(8,128)(2,1)}, u32[]{:S(2)}) copy-start(bf16[1,4,8,32,1024]{4,3,2,1,0:T(8,128)(2,1)} %get-tuple-element.505) | copy-start | bytes 6291460
  517.7 11.0 copy-start.29
  864.4 914.3 %copy-start.28 = (f32[128,1024]{1,0:T(8,128)S(1)}, f32[128,1024]{1,0:T(8,128)}, u32[]{:S(2)}) copy-start(f32[128,1024]{1,0:T(8,128)} %get-tuple-element.245) | copy-start | bytes 1572868
  (60 other events, 108.0 us)
Sparse Core Ops, SparseCore 0:
  256.2 17.9 all-gather.4
  368.6 25.3 reduce-scatter.16
  415.7 133.7 reduce-scatter.32
  551.6 129.9 reduce-scatter.34
  683.8 178.7 reduce-scatter.26
  865.4 142.3 reduce-scatter.24
  1010.8 136.7 reduce-scatter.20
  1150.5 136.8 reduce-scatter.22
  1290.4 144.7 reduce-scatter.30
  1442.6 151.2 reduce-scatter.18
  1596.8 181.8 reduce-scatter.28

commit v2 on v1

v2 whole, which is shorter than its diff:
```python
import functools
from types import SimpleNamespace

import jax
import jax.numpy as jnp
from jax import lax
from jax.experimental import pallas as pl
from jax.experimental.pallas import tpu as pltpu
from jax.sharding import PartitionSpec as P

MESH = pl.DeviceIdType.MESH
F32 = jnp.float32
BF16 = jnp.bfloat16
HEAD_DIM = 64
LANES = 128
TILE = 256


def dot(a, b):
    return jnp.dot(a, b, preferred_element_type=F32)


def dot_nt(a, b):
    return lax.dot_general(a, b, (((1,), (1,)), ((), ())), preferred_element_type=F32)


def place():
    dp, fr = lax.axis_index("dp"), lax.axis_index("frames")
    z, y = lax.div(dp, 2), lax.rem(dp, 2)
    x, c = lax.div(fr, 2), lax.rem(fr, 2)

    def dev(zz, yy, xx, cc):
        return {"dp": zz * 2 + yy, "frames": xx * 2 + cc}

    me = SimpleNamespace(z=z, y=y, x=x, c=c, fr=fr, dev=dev)
    me.xn = dev(z, y, 1 - x, c)
    me.yn = dev(z, 1 - y, x, c)
    me.sib = dev(z, y, x, 1 - c)
    me.diag = dev(z, y, 1 - x, 1 - c)
    return me


def remote(src, dst, send, recv, device):
    return pltpu.make_async_remote_copy(
        src_ref=src, dst_ref=dst, send_sem=send, recv_sem=recv, device_id=device, device_id_type=MESH
    )


def gather_steps(me, w, send, recv, nz):
    half = w.shape[4] // 2
    xo, yo, co = 1 - me.x, 1 - me.y, 1 - me.c

    def cp(view, s, device):
        return remote(view, view, send.at[s], recv.at[s], device)

    def spot(y, x, c):
        return w.at[:, y, x, c]

    def own(z):
        return w.at[z, me.y, me.x, me.c]

    def part(y, x, lower):
        return w.at[:, y, x, me.c, 0:half] if lower else w.at[:, y, x, me.c, half:]

    def step_z():
        for dz in range(1, nz):
            cp(own(me.z), dz - 1, me.dev(lax.rem(me.z + dz, nz), me.y, me.x, me.c)).start()

    def step_near():
        for dz in range(1, nz):
            cp(own(lax.rem(me.z + nz - dz, nz)), dz - 1, me.xn).wait_recv()
        cp(spot(me.y, me.x, me.c), nz - 1, me.xn).start()
        cp(spot(me.y, me.x, me.c), nz, me.yn).start()
        cp(spot(me.y, me.x, me.c), nz + 1, me.sib).start()

    def step_far():
        cp(spot(me.y, xo, me.c), nz - 1, me.xn).wait_recv()
        cp(part(me.y, xo, True), nz + 2, me.yn).start()
        cp(spot(me.y, xo, me.c), nz + 3, me.sib).start()
        cp(spot(yo, me.x, me.c), nz, me.yn).wait_recv()
        cp(part(yo, me.x, False), nz + 4, me.xn).start()
        cp(spot(yo, me.x, me.c), nz + 5, me.sib).start()

    def step_last():
        cp(part(yo, xo, True), nz + 2, me.yn).wait_recv()
        cp(part(yo, xo, False), nz + 4, me.xn).wait_recv()
        cp(spot(yo, xo, me.c), nz + 6, me.sib).start()

    def step_done():
        for y, x, s in ((me.y, me.x, nz + 1), (me.y, xo, nz + 3), (yo, me.x, nz + 5), (yo, xo, nz + 6)):
            cp(spot(y, x, co), s, me.sib).wait_recv()

    def drain():
        for dz in range(1, nz):
            cp(own(me.z), dz - 1, me.xn).wait_send()
        for y, x, s in (
            (me.y, me.x, nz - 1),
            (me.y, me.x, nz),
            (me.y, me.x, nz + 1),
            (me.y, xo, nz + 3),
            (yo, me.x, nz + 5),
            (yo, xo, nz + 6),
        ):
            cp(spot(y, x, me.c), s, me.xn).wait_send()
        cp(part(me.y, xo, True), nz + 2, me.xn).wait_send()
        cp(part(yo, me.x, False), nz + 4, me.xn).wait_send()

    return SimpleNamespace(z=step_z, near=step_near, far=step_far, last=step_last, done=step_done, drain=drain)


def scatter_steps(me, w, box, send, recv, credit, nz, turn, slots, turns, sink):
    half = w.shape[4] // 2
    xo, yo, co = 1 - me.x, 1 - me.y, 1 - me.c
    slot = turn % slots
    core, y1, x1, x2, y2, zs = (b.at[slot] for b in box)

    def above(dz):
        return me.dev(lax.rem(me.z + dz, nz), me.y, me.x, me.c)

    def below(dz):
        return me.dev(lax.rem(me.z + nz - dz, nz), me.y, me.x, me.c)

    moves = [
        (w.at[:, :, :, co], core, me.sib, me.sib),
        (w.at[:, yo, :, me.c, 0:half], y1, me.yn, me.yn),
        (w.at[:, :, xo, me.c, half:], x1, me.xn, me.xn),
        (w.at[:, me.y, xo, me.c, 0:half], x2, me.xn, me.xn),
        (w.at[:, yo, me.x, me.c, half:], y2, me.yn, me.yn),
    ]
    for dz in range(1, nz):
        moves.append((w.at[lax.rem(me.z + dz, nz), me.y, me.x, me.c], zs.at[dz - 1], above(dz), below(dz)))

    def cp(i):
        src, dst, to, _ = moves[i]
        return remote(src, dst, send.at[i], recv.at[i], to)

    def go(i):
        if turn >= slots:
            pl.semaphore_wait(credit.at[i], 1)
        cp(i).start()

    def free(i):
        if turn + slots < turns:
            pl.semaphore_signal(credit.at[i], inc=1, device_id=moves[i][3], device_id_type=MESH)

    def add(view, arrived):
        view[...] = (view[...].astype(F32) + arrived[...].astype(F32)).astype(w.dtype)

    def step_a():
        go(0)

    def step_b():
        cp(0).wait_recv()

        def body(zz, carry):
            for y in range(2):
                for x in range(2):
                    add(w.at[zz, y, x, me.c], core.at[zz, y, x])
            return carry

        lax.fori_loop(0, nz, body, 0)
        free(0)
        go(1)
        go(2)

    def step_c():
        cp(1).wait_recv()
        cp(2).wait_recv()

        def body(zz, carry):
            for o in range(2):
                add(w.at[zz, me.y, o, me.c, 0:half], y1.at[zz, o])
                add(w.at[zz, o, me.x, me.c, half:], x1.at[zz, o])
            return carry

        lax.fori_loop(0, nz, body, 0)
        free(1)
        free(2)
        go(3)
        go(4)

    def step_d():
        cp(3).wait_recv()
        cp(4).wait_recv()

        def body(zz, carry):
            add(w.at[zz, me.y, me.x, me.c, 0:half], x2.at[zz])
            add(w.at[zz, me.y, me.x, me.c, half:], y2.at[zz])
            return carry

        lax.fori_loop(0, nz, body, 0)
        free(3)
        free(4)
        for dz in range(1, nz):
            go(4 + dz)

    def step_e():
        total = w[me.z, me.y, me.x, me.c].astype(F32)
        for dz in range(1, nz):
            cp(4 + dz).wait_recv()
            total = total + zs[dz - 1].astype(F32)
        sink(total)
        for dz in range(1, nz):
            free(4 + dz)

    def drain():
        for i in range(len(moves)):
            cp(i).wait_send()

    return SimpleNamespace(a=step_a, b=step_b, c=step_c, d=step_d, e=step_e, drain=drain)


def lane_masks():
    lane = lax.broadcasted_iota(jnp.int32, (1, LANES), 1)
    left = jnp.where(lane < HEAD_DIM, 1.0, 0.0).astype(BF16)
    return left, (1.0 - left.astype(F32)).astype(BF16)


def two_heads(block):
    left, right = lane_masks()
    return jnp.concatenate([block * left, block * right], axis=0)


def one_block(pair):
    rows = pair.shape[0] // 2
    lane = lax.broadcasted_iota(jnp.int32, (rows, LANES), 1)
    return jnp.where(lane < HEAD_DIM, pair[:rows], pair[rows:])


def at128(p, base=0):
    return pl.ds(pl.multiple_of(base + p * LANES, LANES), LANES)


def put_stat(stat, p, pair):
    rows = pair.shape[0] // 2
    lane = lax.broadcasted_iota(jnp.int32, stat.shape, 1)
    stat = jnp.where(lane == 2 * p, pair[:rows], stat)
    return jnp.where(lane == 2 * p + 1, pair[rows:], stat)


def normalise(values):
    center = values - jnp.mean(values, axis=-1, keepdims=True)
    spread = jnp.mean(center * center, axis=-1, keepdims=True)
    return center * lax.rsqrt(spread + 1e-05)


def forward(r, me, nz):
    rows, d = r.tokens.shape
    items, frames = r.kv.shape[:2]
    pairs = d // LANES

    def weight(k, n):
        return r.wg[k, :, :, :, :, :, pl.ds(pl.multiple_of(n * TILE, TILE), TILE)].reshape(d, TILE)

    def product(x, k, sink):
        def body(n, carry):
            sink(n, pl.ds(pl.multiple_of(n * TILE, TILE), TILE), dot(x, weight(k, n)))
            return carry

        lax.fori_loop(0, d // TILE, body, 0)

    def ln(values, i):
        return normalise(values) * r.gs[i : i + 1, :] + r.gs[4 + i : 5 + i, :]

    def norms_in():
        for g in range(2 * nz):
            total = r.ng[g // 2, g % 2, 0, 0, 0:16, :].astype(F32)
            for f in range(1, 4):
                total = total + r.ng[g // 2, g % 2, f // 2, f % 2, 0:16, :].astype(F32)
            r.gs[:, g * LANES : (g + 1) * LANES] = total

    def norm_one():
        pltpu.make_async_copy(r.tokens, r.first, r.own_sem.at[1]).wait()
        r.xb[...] = ln(r.first[...], 0).astype(BF16)
        r.n1t[...] = r.xb[...].T

    def joint(q):
        def sink(n, cols, v):
            r.joint[:, pl.ds(pl.multiple_of(q * d + n * TILE, TILE), TILE)] = v.astype(BF16)

        product(r.xb[...], q, sink)

    def self_attention():
        row = lax.rem(lax.broadcasted_iota(jnp.int32, (2 * rows, rows), 0), rows)
        causal = row >= lax.broadcasted_iota(jnp.int32, (2 * rows, rows), 1)

        def body(p, stat):
            q2 = two_heads(r.joint[:, at128(p)] * jnp.asarray(HEAD_DIM**-0.5, BF16))
            s = dot_nt(q2, r.joint[:, at128(p, d)])
            s = jnp.where(causal, s, -1e30)
            m = jnp.max(s, axis=-1, keepdims=True)
            e = jnp.exp(s - m)
            total = jnp.sum(e, axis=-1, keepdims=True)
            o2 = dot(e.astype(BF16), r.joint[:, at128(p, 2 * d)]) / total
            r.xb[:, at128(p)] = one_block(o2).astype(BF16)
            return put_stat(stat, p, m + jnp.log(total))

        stat = lax.fori_loop(0, pairs, body, jnp.zeros((rows, LANES), F32))
        r.slse[...] = stat.T
        r.smixt[...] = r.xb[...].T

    def self_out():
        def sink(n, cols, v):
            r.branch[:, cols] = v

        product(r.xb[...], 3, sink)
        r.first[...] = r.first[...] + r.branch[...]
        squares(1, r.branch[...])
        r.xb[...] = ln(r.first[...], 1).astype(BF16)
        r.n2t[...] = r.xb[...].T

    def squares(i, values):
        ok = lax.broadcasted_iota(jnp.int32, (rows, 1), 0) < r.tl[0]
        total = jnp.sum(jnp.where(ok, values * values, 0.0))
        line = lax.broadcasted_iota(jnp.int32, r.sq.shape, 0)
        r.sq[...] = jnp.where(line == i, total, r.sq[...])

    def start_counts():
        line = lax.broadcasted_iota(jnp.int32, r.sq.shape, 0)
        r.sq[...] = jnp.where(line == 4, r.tl[0].astype(F32), 0.0)

    def queries():
        def sink(n, cols, v):
            r.qa[me.fr, :, cols] = v.astype(BF16)

        product(r.xb[...], 4, sink)

    def q_copy(f, s, device):
        return remote(r.qa.at[f], r.qa.at[f], r.q_send.at[s], r.q_recv.at[s], device)

    fx, fs, fd = (1 - me.x) * 2 + me.c, me.x * 2 + 1 - me.c, (1 - me.x) * 2 + 1 - me.c

    def q_start():
        q_copy(me.fr, 0, me.xn).start()
        q_copy(me.fr, 1, me.sib).start()

    def q_forward():
        q_copy(fx, 0, me.xn).wait_recv()
        q_copy(fx, 2, me.sib).start()

    def q_done():
        q_copy(fs, 1, me.sib).wait_recv()
        q_copy(fd, 2, me.sib).wait_recv()

    def mem_copy(t):
        return pltpu.make_async_copy(r.memory.at[t], r.rc.at[t % 2, 0 : r.memory.shape[1]], r.m_sem.at[t % 2])

    def memory_part(which):
        def item(t):
            mem_copy(t).wait()
            stage = r.rc.at[t % 2, 0 : r.memory.shape[1]]

            def body(n, carry):
                v = dot(stage[...].reshape(frames, d), weight(5 + which, n))
                r.kv[t, :, pl.ds(pl.multiple_of(which * d + n * TILE, TILE), TILE)] = v.astype(BF16)
                return carry

            lax.fori_loop(0, d // TILE, body, 0)
            if which == 0:
                r.memt[:, t * frames : (t + 1) * frames] = stage[...].reshape(frames, d).T
            if t + 2 < items:
                mem_copy(t + 2).start()

        def run():
            for t in range(items):
                item(t)
            if which == 0:
                for t in range(min(2, items)):
                    mem_copy(t).start()

        return run

    def mem_start():
        for t in range(min(2, items)):
            mem_copy(t).start()

    def cross_item(t):
        def body(p, stat):
            q2 = two_heads(r.qa[t, :, at128(p)] * jnp.asarray(HEAD_DIM**-0.5, BF16))
            s = dot_nt(q2, r.kv[t, :, at128(p)]) + r.bias[pl.ds(t, 1), :]
            m = jnp.max(s, axis=-1, keepdims=True)
            e = jnp.exp(s - m)
            total = jnp.sum(e, axis=-1, keepdims=True)
            o2 = dot(e.astype(BF16), r.kv[t, :, at128(p, d)]) / total
            r.op[t, :, at128(p)] = one_block(o2).astype(BF16)
            return put_stat(stat, p, m + jnp.log(total))

        stat = lax.fori_loop(0, pairs, body, jnp.zeros((rows, LANES), F32))
        r.opl[t] = stat.T

    def o_copies(t, slot, device):
        return (
            remote(r.op.at[t], r.orv.at[slot], r.o_send.at[slot], r.o_recv.at[slot], device),
            remote(r.opl.at[t, 0:16], r.orl.at[slot, 0:16], r.o_send.at[3 + slot], r.o_recv.at[3 + slot], device),
        )

    def o_start(t, slot, device):
        for cp in o_copies(t, slot, device):
            cp.start()

    def o_wait(t, slot, device):
        for cp in o_copies(t, slot, device):
            cp.wait_recv()

    def merge(parts, sink):
        lses = [lse[0:16] for _, lse in parts]
        top = functools.reduce(jnp.maximum, lses)
        shares = [jnp.exp(v - top) for v in lses]
        total = functools.reduce(jnp.add, shares)
        flat = jnp.concatenate([v / total for v in shares] + [jnp.zeros((LANES - 16 * len(parts), LANES), F32)], axis=0)
        r.wcol[...] = flat.T
        lane = lax.broadcasted_iota(jnp.int32, (rows, LANES), 1)
        for p in range(pairs):
            value = jnp.zeros((rows, LANES), F32)
            for i, (mix, _) in enumerate(parts):
                left = r.wcol[:, 16 * i + 2 * p : 16 * i + 2 * p + 1]
                right = r.wcol[:, 16 * i + 2 * p + 1 : 16 * i + 2 * p + 2]
                share = jnp.where(lane < HEAD_DIM, left, right)
                value = value + share * mix[:, p * LANES : (p + 1) * LANES].astype(F32)
            sink(p, value)
        return top + jnp.log(total)

    def cross_a():
        cross_item(fd)
        o_start(fd, 0, me.sib)
        cross_item(fs)
        o_start(fs, 1, me.sib)

    def cross_b():
        cross_item(fx)
        o_wait(fd, 0, me.sib)

        def sink(p, v):
            r.op[fx, :, p * LANES : (p + 1) * LANES] = v.astype(BF16)

        lse = merge([(r.op.at[fx], r.opl.at[fx]), (r.orv.at[0], r.orl.at[0])], sink)
        r.opl[fx, 0:16] = lse
        o_start(fx, 2, me.xn)
        cross_item(me.fr)

    def cross_c():
        o_wait(fs, 1, me.sib)
        o_wait(fx, 2, me.xn)

        def sink(p, v):
            r.xb[:, p * LANES : (p + 1) * LANES] = v.astype(BF16)

        parts = [(r.op.at[me.fr], r.opl.at[me.fr]), (r.orv.at[1], r.orl.at[1]), (r.orv.at[2], r.orl.at[2])]
        r.clse[0:16] = merge(parts, sink)
        r.cmixt[...] = r.xb[...].T

    def cross_out():
        def sink(n, cols, v):
            r.branch[:, cols] = v

        product(r.xb[...], 7, sink)
        squares(2, r.branch[...])
        r.second[...] = r.first[...] + r.branch[...]
        r.xb[...] = ln(r.second[...], 2).astype(BF16)
        r.n3t[...] = r.xb[...].T

    def expand(q):
        def sink(n, cols, v):
            at = pl.ds(pl.multiple_of(q * d + n * TILE, TILE), TILE)
            half = 0.5 * (1.0 + lax.erf(v * (2.0**-0.5)))
            r.active[:, at] = (v * half).astype(BF16)
            r.slope[:, at] = (half + v * jnp.exp(-0.5 * v * v) * 0.3989422804014327).astype(BF16)

        product(r.xb[...], 8 + q, sink)
        r.activet[q * d : (q + 1) * d, :] = r.active[:, q * d : (q + 1) * d].T

    def contract(q):
        def sink(n, cols, v):
            r.branch[:, cols] = v if q == 0 else r.branch[:, cols] + v

        product(r.active[:, q * d : (q + 1) * d], 12 + q, sink)

    def finish():
        squares(3, r.branch[...])
        r.third[...] = r.second[...] + r.branch[...]
        squares(0, r.third[...])
        ok = lax.broadcasted_iota(jnp.int32, (rows, 1), 0) < r.tl[0]
        r.result[...] = jnp.where(ok, ln(r.third[...], 3), 0.0)

    def at(k):
        return k + 3

    tasks = {}

    def add(tick, *fs):
        tasks.setdefault(tick, []).extend(fs)

    add(0, start_counts, mem_start)
    add(2, norms_in, norm_one)
    for q in range(3):
        add(at(q), functools.partial(joint, q))
    add(at(2), self_attention)
    add(at(3), self_out)
    add(at(4), queries, q_start)
    add(at(5), q_forward, memory_part(0))
    add(at(6), memory_part(1), q_done, cross_a)
    add(at(7), cross_b)
    add(at(8), cross_c, cross_out)
    for q in range(4):
        add(at(8 + q), functools.partial(expand, q))
        add(at(12 + q), functools.partial(contract, q))
    add(at(15), finish)

    def drain():
        q_copy(me.fr, 0, me.xn).wait_send()
        q_copy(me.fr, 1, me.sib).wait_send()
        q_copy(fx, 2, me.sib).wait_send()
        for t, slot, device in ((fd, 0, me.sib), (fs, 1, me.sib), (fx, 2, me.xn)):
            for cp in o_copies(t, slot, device):
                cp.wait_send()

    return tasks, drain, (fx, fs, fd)


def ln_back(values, gain_row, grad):
    center = values - jnp.mean(values, axis=-1, keepdims=True)
    scale = lax.rsqrt(jnp.mean(center * center, axis=-1, keepdims=True) + 1e-05)
    unit = center * scale
    gain_grad = jnp.sum(grad * unit, axis=0, keepdims=True)
    shift_grad = jnp.sum(grad, axis=0, keepdims=True)
    lifted = grad * gain_row
    inner = jnp.mean(lifted * unit, axis=-1, keepdims=True)
    back = scale * (lifted - jnp.mean(lifted, axis=-1, keepdims=True) - unit * inner)
    return back, gain_grad, shift_grad


def backward(r, me, nz, fronts):
    rows, d = r.first.shape
    items, frames = r.kv.shape[:2]
    pairs = d // LANES
    depth = d // nz
    fx, fs, fd = fronts
    t = {}

    def cols(n):
        return pl.ds(pl.multiple_of(n * TILE, TILE), TILE)

    def weight_rows(k, zz):
        return r.wg[k, zz].reshape(depth, d)

    def grad_into(k, left, right):
        def body(n, carry):
            v = dot(left, right(cols(n))).astype(BF16)
            r.wg[k, :, :, :, :, :, cols(n)] = v.reshape(nz, 2, 2, 2, d // (8 * nz), TILE)
            return carry

        lax.fori_loop(0, d // TILE, body, 0)

    def through(k, grad, sink):
        def body(zz, carry):
            sink(zz, pl.ds(pl.multiple_of(zz * depth, depth), depth), dot_nt(grad, weight_rows(k, zz)))
            return carry

        lax.fori_loop(0, nz, body, 0)

    def ln_step(i, values, grad, first=False):
        back, gain, shift = ln_back(values, r.gs[i : i + 1, :], grad)
        r.gr[...] = back if first else r.gr[...] + back
        r.nrow[i : i + 1, :] = gain
        r.nrow[4 + i : 5 + i, :] = shift

    def start():
        pltpu.make_async_copy(r.cotangent, r.gr, r.own_sem.at[2]).wait()
        r.biast[...] = jnp.concatenate([r.bias[...], jnp.zeros((LANES - r.bias.shape[0], frames), F32)], axis=0).T
        for g in range(d // LANES):
            r.nrow[8:16, g * LANES : (g + 1) * LANES] = r.sq[...]
        ok = lax.broadcasted_iota(jnp.int32, (rows, 1), 0) < r.tl[0]
        ln_step(3, r.third[...], jnp.where(ok, r.gr[...], 0.0), True)
        r.xb[...] = r.gr[...].astype(BF16)
        pltpu.make_async_copy(r.tokens, r.third, r.own_sem.at[1]).start()

    def contract(q):
        def sink(zz, at, v):
            at = pl.ds(pl.multiple_of(q * d + zz * depth, depth), depth)
            r.active[:, at] = (v * r.slope[:, at].astype(F32)).astype(BF16)

        through(12 + q, r.xb[...], sink)
        grad_into(12 + q, r.activet[q * d : (q + 1) * d, :], lambda at: r.xb[:, at])

    def adder(fresh):
        def sink(zz, at, v):
            r.branch[:, at] = v if fresh else r.branch[:, at] + v

        return sink

    def expand(q):
        through(8 + q, r.active[:, q * d : (q + 1) * d], adder(q == 0))
        grad_into(8 + q, r.n3t[...], lambda at: r.active[:, pl.ds(pl.multiple_of(q * d + at.start, TILE), TILE)])

    def cross_out():
        ln_step(2, r.second[...], r.branch[...])
        r.xb[...] = r.gr[...].astype(BF16)

        def sink(zz, at, v):
            r.ga[me.fr, :, at] = v.astype(BF16)

        through(7, r.xb[...], sink)
        r.gl[me.fr, 0:16] = r.clse[0:16]

        def body(p, carry):
            left, right = row_dots(r.ga[me.fr, :, at128(p)], r.cmixt[at128(p), :])
            r.gl[me.fr, pl.ds(16 + 2 * p, 1), :] = left
            r.gl[me.fr, pl.ds(17 + 2 * p, 1), :] = right
            return carry

        lax.fori_loop(0, pairs, body, 0)

    def cross_out_grad():
        grad_into(7, r.cmixt[...], lambda at: r.xb[:, at])

    def row_dots(grad, mixt):
        prod = grad.astype(F32).T * mixt.astype(F32)
        return jnp.sum(prod[:HEAD_DIM], axis=0, keepdims=True), jnp.sum(prod[HEAD_DIM:], axis=0, keepdims=True)

    def g_copies(f, s, device):
        return (
            remote(r.ga.at[f], r.ga.at[f], r.g2_send.at[s], r.g2_recv.at[s], device),
            remote(r.gl.at[f], r.gl.at[f], r.g2_send.at[3 + s], r.g2_recv.at[3 + s], device),
        )

    def each(copies, what):
        for cp in copies:
            getattr(cp, what)()

    def g_start():
        each(g_copies(me.fr, 0, me.xn), "start")
        each(g_copies(me.fr, 1, me.sib), "start")

    def g_forward():
        each(g_copies(fx, 0, me.xn), "wait_recv")
        each(g_copies(fx, 2, me.sib), "start")

    def g_drain():
        each(g_copies(me.fr, 0, me.xn), "wait_send")
        each(g_copies(me.fr, 1, me.sib), "wait_send")
        each(g_copies(fx, 2, me.sib), "wait_send")

    scale = HEAD_DIM**-0.5

    def pair_back(q, k, v, g, hide, lse, dots):
        q2, g2 = two_heads(q * jnp.asarray(scale, BF16)), two_heads(g)
        probs = jnp.exp(hide(dot_nt(k, q2)) - lse)
        ds = (probs * (dot_nt(v, g2) - dots)).astype(BF16)
        dq = one_block(dot(ds.T, k)) * scale
        return dq, dot(ds, q2), dot(probs.astype(BF16), g2)

    def cross_item(f):
        lane = lax.broadcasted_iota(jnp.int32, (frames, LANES), 1)
        column = jnp.sum(jnp.where(lane == f, r.biast[...], 0.0), axis=-1, keepdims=True)

        def body(p, carry):
            stats = [
                jnp.concatenate([r.gl[f, pl.ds(b + 2 * p, 1), :], r.gl[f, pl.ds(b + 1 + 2 * p, 1), :]], axis=1)
                for b in (0, 16)
            ]
            dq, dk, dv = pair_back(
                r.qa[f, :, at128(p)],
                r.kv[f, :, at128(p)],
                r.kv[f, :, at128(p, d)],
                r.ga[f, :, at128(p)],
                lambda s: s + column,
                *stats,
            )
            r.op[f, :, at128(p)] = dq.astype(BF16)
            r.kv[f, :, at128(p)] = dk.astype(BF16)
            r.kv[f, :, at128(p, d)] = dv.astype(BF16)
            return carry

        lax.fori_loop(0, pairs, body, 0)

    def d_copy(f, slot, device):
        return remote(r.op.at[f], r.orv.at[slot], r.o2_send.at[slot], r.o2_recv.at[slot], device)

    def cross_one():
        cross_item(me.fr)

    def cross_two():
        each(g_copies(fs, 1, me.sib), "wait_recv")
        cross_item(fs)
        d_copy(fs, 1, me.sib).start()

    def cross_three():
        each(g_copies(fd, 2, me.sib), "wait_recv")
        cross_item(fd)
        d_copy(fd, 0, me.sib).start()

    def cross_four():
        cross_item(fx)
        d_copy(fd, 0, me.sib).wait_recv()
        r.op[fx] = (r.op[fx].astype(F32) + r.orv[0].astype(F32)).astype(BF16)
        d_copy(fx, 2, me.xn).start()

    def tile_copy(i, f, zz):
        return pltpu.make_async_copy(
            r.mst.at[i, 0 : r.memory_grad.shape[1]],
            r.memory_grad.at[f, :, pl.ds(pl.multiple_of(zz * depth, depth), depth)],
            r.t_sem.at[i],
        )

    def memory_grad(half):
        def body(n, carry):
            f, pair = lax.div(n, nz // 2), lax.rem(n, nz // 2)
            for i in range(2):
                zz = 2 * pair + i

                @pl.when(n > half * items * nz // 4)
                def _():
                    tile_copy(i, f, zz).wait()

                v = dot_nt(r.kv[f, :, 0:d], weight_rows(5, zz)) + dot_nt(r.kv[f, :, d : 2 * d], weight_rows(6, zz))
                r.mst[i] = v
                tile_copy(i, f, zz).start()
            return carry

        count = items * nz // 4
        lax.fori_loop(half * count, (half + 1) * count, body, 0)
        for i in range(2):
            tile_copy(i, 0, i).wait()

    def memory_weights(which):
        grad_into(
            5 + which,
            r.memt[...],
            lambda at: r.kv[:, :, pl.ds(pl.multiple_of(which * d + at.start, TILE), TILE)].reshape(items * frames, TILE),
        )

    def query():
        d_copy(fs, 1, me.sib).wait_recv()
        d_copy(fx, 2, me.xn).wait_recv()
        r.xb[...] = (r.op[me.fr].astype(F32) + r.orv[1].astype(F32) + r.orv[2].astype(F32)).astype(BF16)
        through(4, r.xb[...], adder(True))
        grad_into(4, r.n2t[...], lambda at: r.xb[:, at])

    def d_drain():
        for f, slot, device in ((fd, 0, me.sib), (fs, 1, me.sib), (fx, 2, me.xn)):
            d_copy(f, slot, device).wait_send()

    def self_out():
        ln_step(1, r.first[...], r.branch[...])
        r.xb[...] = r.gr[...].astype(BF16)

        def sink(zz, at, v):
            r.ga[me.fr, :, at] = v.astype(BF16)

        through(3, r.xb[...], sink)
        grad_into(3, r.smixt[...], lambda at: r.xb[:, at])

    def self_attention():
        key = lax.broadcasted_iota(jnp.int32, (rows, 2 * rows), 0)
        causal = key <= lax.rem(lax.broadcasted_iota(jnp.int32, (rows, 2 * rows), 1), rows)

        def body(p, carry):
            g = r.ga[me.fr, :, at128(p)]
            lse = jnp.concatenate([r.slse[pl.ds(2 * p, 1), :], r.slse[pl.ds(2 * p + 1, 1), :]], axis=1)
            dots = jnp.concatenate(row_dots(g, r.smixt[at128(p), :]), axis=1)
            dq, dk, dv = pair_back(
                r.joint[:, at128(p)],
                r.joint[:, at128(p, d)],
                r.joint[:, at128(p, 2 * d)],
                g,
                lambda s: jnp.where(causal, s, -1e30),
                lse,
                dots,
            )
            r.joint[:, at128(p)] = dq.astype(BF16)
            r.joint[:, at128(p, d)] = dk.astype(BF16)
            r.joint[:, at128(p, 2 * d)] = dv.astype(BF16)
            return carry

        lax.fori_loop(0, pairs, body, 0)

    def project(q):
        through(q, r.joint[:, q * d : (q + 1) * d], adder(q == 0))
        grad_into(q, r.n1t[...], lambda at: r.joint[:, pl.ds(pl.multiple_of(q * d + at.start, TILE), TILE)])

    def finish():
        pltpu.make_async_copy(r.tokens, r.third, r.own_sem.at[1]).wait()
        ln_step(0, r.third[...], r.branch[...])
        pltpu.make_async_copy(r.gr, r.tokens_grad, r.own_sem.at[2]).start()
        for g in range(d // LANES):
            for f in range(4):
                r.nw[g // 2, g % 2, f // 2, f % 2] = r.nrow[:, g * LANES : (g + 1) * LANES]

    def close():
        pltpu.make_async_copy(r.gr, r.tokens_grad, r.own_sem.at[2]).wait()

    return SimpleNamespace(**{k: v for k, v in locals().items() if callable(v)})


GRAD_ORDER = (12, 13, 14, 15, 8, 9, 10, 11, 7, 5, 6, 4, 3, 0, 1, 2)
SLOTS = 2


def run(r, nz, chunks):
    me = place()
    own = pltpu.make_async_copy(r.shards, r.wg.at[:, me.z, me.y, me.x, me.c], r.own_sem.at[0])
    own.start()
    pltpu.make_async_copy(r.tokens, r.first, r.own_sem.at[1]).start()
    pltpu.make_async_copy(r.cotangent, r.gr, r.own_sem.at[2]).start()
    r.ng[me.z, me.y, me.x, me.c] = r.norms[...]
    barrier = pltpu.get_barrier_semaphore()
    peers = [me.xn, me.yn, me.sib, me.diag]
    peers += [me.dev(lax.rem(me.z + dz, nz), me.y, me.x, me.c) for dz in range(1, nz)]
    for device in peers:
        pl.semaphore_signal(barrier, inc=1, device_id=device, device_id_type=MESH)
    pl.semaphore_wait(barrier, len(peers))
    norm = gather_steps(me, r.ng, r.g_send.at[chunks], r.g_recv.at[chunks], nz)
    steps = [gather_steps(me, r.wg.at[k], r.g_send.at[k], r.g_recv.at[k], nz) for k in range(chunks)]
    norm.z()
    own.wait()
    steps[0].z()
    steps[1].z()
    norm.near()
    norm.far()
    norm.last()
    tasks, drain, fronts = forward(r, me, nz)
    for tick in range(chunks + 3):
        if tick + 2 < chunks:
            steps[tick + 2].z()
        if tick < chunks:
            steps[tick].near()
        if 0 <= tick - 1 < chunks:
            steps[tick - 1].far()
        if 0 <= tick - 2 < chunks:
            steps[tick - 2].last()
        if 0 <= tick - 3 < chunks:
            steps[tick - 3].done()
        if tick == 1:
            norm.done()
        for task in tasks.get(tick, ()):
            task()
    drain()
    norm.drain()
    for s in steps:
        s.drain()

    b = backward(r, me, nz, fronts)

    def out_copy(turn):
        return pltpu.make_async_copy(r.ost.at[turn % 2], r.grads.at[GRAD_ORDER[turn]], r.e_sem.at[turn % 2])

    def keep(turn):
        def sink(total):
            if turn >= 2:
                out_copy(turn - 2).wait()
            r.ost[turn % 2] = total
            out_copy(turn).start()

        return sink

    def keep_norms(total):
        r.norm_out[...] = total

    boxes = (r.rc, r.y1, r.x1, r.x2, r.y2, r.zs)
    adds = [
        scatter_steps(me, r.wg.at[k], boxes, r.s_send.at[m], r.s_recv.at[m], r.credit, nz, m, SLOTS, chunks, keep(m))
        for m, k in enumerate(GRAD_ORDER)
    ]
    norm_boxes = (r.nrc, r.ny1, r.nx1, r.nx2, r.ny2, r.nzs)
    adds.append(
        scatter_steps(me, r.nw, norm_boxes, r.s_send.at[chunks], r.s_recv.at[chunks], r.credit, nz, 0, 1, 1, keep_norms)
    )
    part = functools.partial
    work = {
        -1: [b.start, part(b.contract, 0)],
        0: [part(b.contract, 1)],
        1: [part(b.contract, 2), part(b.contract, 3)],
        2: [part(b.expand, 0), part(b.expand, 1)],
        3: [part(b.expand, 2), part(b.expand, 3)],
        4: [b.cross_out, b.g_start, b.cross_out_grad, b.cross_one],
        5: [b.g_forward, b.cross_two, b.cross_three],
        6: [b.cross_four, b.g_drain, part(b.memory_grad, 0)],
        7: [part(b.memory_grad, 1), part(b.memory_weights, 0)],
        8: [part(b.memory_weights, 1), b.query],
        9: [b.d_drain, b.self_out],
        10: [b.self_attention, part(b.project, 0)],
        11: [part(b.project, 1), part(b.project, 2)],
        12: [b.finish],
    }
    extra = chunks + 1
    for tick in range(-1, extra + 3):
        for task in work.get(tick, ()):
            task()
        if tick + 1 < extra:
            adds[tick + 1].a()
        if 0 <= tick < extra:
            adds[tick].b()
        if 0 <= tick - 1 < extra:
            adds[tick - 1].c()
        if 0 <= tick - 2 < extra:
            adds[tick - 2].d()
        if 0 <= tick - 3 < extra:
            adds[tick - 3].e()
    b.close()
    out_copy(chunks - 2).wait()
    out_copy(chunks - 1).wait()
    for s in adds:
        s.drain()


VMEM_BYTES = 127 * 2**19


def fused(nz, chunks, frame_count, tl, tokens, cotangent, memory, shards, norms, bias):
    rows, d = tokens.shape
    items, parts = memory.shape[0], memory.shape[1]
    slab = shards.shape[1]
    padded = parts * 4 * slab
    half = slab // 2
    outs = dict(
        result=((rows, d), F32, pltpu.VMEM),
        tokens_grad=((rows, d), F32, pl.ANY),
        memory_grad=((items, frame_count, d), F32, pl.ANY),
        grads=((chunks, slab, d), F32, pl.ANY),
        norm_out=((16, LANES), F32, pltpu.VMEM),
    )
    vm = pltpu.VMEM
    dma = pltpu.SemaphoreType.DMA
    scratch = dict(
        wg=vm((chunks, nz, 2, 2, 2, slab, d), BF16),
        ng=vm((nz, 2, 2, 2, 32, LANES), BF16),
        gs=vm((16, d), F32),
        n1t=vm((d, rows), BF16),
        joint=vm((rows, 3 * d), BF16),
        smixt=vm((d, rows), BF16),
        slse=vm((LANES, LANES), F32),
        first=vm((rows, d), F32),
        n2t=vm((d, rows), BF16),
        qa=vm((items, rows, d), BF16),
        kv=vm((items, padded, 2 * d), BF16),
        memt=vm((d, items * padded), BF16),
        clse=vm((LANES, LANES), F32),
        second=vm((rows, d), F32),
        n3t=vm((d, rows), BF16),
        activet=vm((4 * d, rows), BF16),
        active=vm((rows, 4 * d), BF16),
        slope=vm((rows, 4 * d), BF16),
        third=vm((rows, d), F32),
        sq=vm((8, LANES), F32),
        xb=vm((rows, d), BF16),
        branch=vm((rows, d), F32),
        op=vm((items, rows, d), BF16),
        opl=vm((items, LANES, LANES), F32),
        orv=vm((3, rows, d), BF16),
        orl=vm((3, LANES, LANES), F32),
        wcol=vm((LANES, LANES), F32),
        cmixt=vm((d, rows), BF16),
        gr=vm((rows, d), F32),
        ga=vm((items, rows, d), BF16),
        gl=vm((items, 32, LANES), F32),
        nrow=vm((16, d), F32),
        biast=vm((padded, LANES), F32),
        mst=vm((2, padded, d // nz), F32),
        ost=vm((2, slab, d), F32),
        nw=vm((nz, 2, 2, 2, 16, LANES), F32),
        rc=vm((SLOTS, nz, 2, 2, slab, d), BF16),
        y1=vm((SLOTS, nz, 2, half, d), BF16),
        x1=vm((SLOTS, nz, 2, half, d), BF16),
        x2=vm((SLOTS, nz, half, d), BF16),
        y2=vm((SLOTS, nz, half, d), BF16),
        zs=vm((SLOTS, nz - 1, slab, d), BF16),
        nrc=vm((1, nz, 2, 2, 16, LANES), F32),
        ny1=vm((1, nz, 2, 8, LANES), F32),
        nx1=vm((1, nz, 2, 8, LANES), F32),
        nx2=vm((1, nz, 8, LANES), F32),
        ny2=vm((1, nz, 8, LANES), F32),
        nzs=vm((1, nz - 1, 16, LANES), F32),
        own_sem=dma((3,)),
        m_sem=dma((2,)),
        t_sem=dma((2,)),
        e_sem=dma((2,)),
        g_send=dma((chunks + 1, nz + 7)),
        g_recv=dma((chunks + 1, nz + 7)),
        s_send=dma((chunks + 1, nz + 4)),
        s_recv=dma((chunks + 1, nz + 4)),
        credit=pltpu.SemaphoreType.REGULAR((nz + 4,)),
        q_send=dma((3,)),
        q_recv=dma((3,)),
        o_send=dma((6,)),
        o_recv=dma((6,)),
        g2_send=dma((6,)),
        g2_recv=dma((6,)),
        o2_send=dma((3,)),
        o2_recv=dma((3,)),
    )
    ins = ["tl", "tokens", "cotangent", "memory", "shards", "norms", "bias"]
    names = ins + list(outs) + list(scratch)

    def kernel(*refs):
        run(SimpleNamespace(**dict(zip(names, refs))), nz, chunks)

    def at(space):
        return pl.BlockSpec(memory_space=space)

    res = pl.pallas_call(
        kernel,
        out_shape=[jax.ShapeDtypeStruct(s, t) for s, t, _ in outs.values()],
        in_specs=[at(s) for s in (pltpu.SMEM, pl.ANY, pl.ANY, pl.ANY, pl.ANY, pltpu.VMEM, pltpu.VMEM)],
        out_specs=[at(s) for _, _, s in outs.values()],
        scratch_shapes=list(scratch.values()),
        compiler_params=pltpu.CompilerParams(collective_id=0, has_side_effects=True, vmem_limit_bytes=VMEM_BYTES),
    )(tl, tokens, cotangent, memory, shards, norms, bias)
    return dict(zip(outs, res))


CHUNKS = 16
Z_CHIPS = 4


def pack_weights(weights):
    self_project, self_output, cross_query, cross_memory, cross_output, expand, contract = weights
    slab, d = self_output.shape
    devices = d // slab
    blocks = contract.shape[0] // slab

    def cut(w):
        return jnp.transpose(w.reshape(slab, -1, d), (1, 0, 2))

    wide = jnp.transpose(expand.reshape(slab, devices, blocks, slab), (2, 0, 1, 3)).reshape(blocks, slab, d)
    return jnp.concatenate(
        [cut(w) for w in (self_project, self_output, cross_query, cross_memory, cross_output)]
        + [wide, contract.reshape(blocks, slab, d)],
        axis=0,
    )


def pack_norms(gains, shifts):
    own = jnp.concatenate([gains, shifts], axis=0)
    lane = lax.axis_index("frames") * own.shape[1]
    return lax.dynamic_update_slice(jnp.zeros((32, LANES), BF16), own, (0, lane))


def frame_bias(cross_mask, memory_length, frame_count, padded):
    start = lax.axis_index("frames") * frame_count
    at = start + jnp.arange(frame_count)
    mask = lax.dynamic_slice_in_dim(cross_mask, start, frame_count, 1)
    ok = (at[None] < memory_length[:, None]) & ((mask == 1) | (at[None] == 0))
    bias = jnp.where(ok, 0.0, -1e30).astype(F32)
    return jnp.pad(bias, ((0, 8 - bias.shape[0]), (0, padded - frame_count)), constant_values=-1e30)


def local_fused(
    tokens,
    memory,
    cotangent,
    self_project,
    self_output,
    cross_query,
    cross_memory,
    cross_output,
    expand,
    contract,
    norm_gains,
    norm_shifts,
    target_length,
    memory_length,
    cross_mask,
):
    items, frame_count, d = memory.shape
    slab = self_output.shape[0]
    group = 4 * slab
    parts = -(-frame_count // group)
    padded = parts * group
    rolled = jnp.pad(memory, ((0, 0), (0, padded - frame_count), (0, 0))).reshape(items, parts, 2, 2, slab, d)
    weights = (self_project, self_output, cross_query, cross_memory, cross_output, expand, contract)
    o = fused(
        Z_CHIPS,
        CHUNKS,
        frame_count,
        target_length,
        tokens[0],
        cotangent[0],
        rolled,
        pack_weights(weights),
        pack_norms(norm_gains, norm_shifts),
        frame_bias(cross_mask, memory_length, frame_count, padded),
    )
    g = o["grads"]
    blocks = contract.shape[0] // slab

    def side(lo, hi):
        return jnp.concatenate([g[k] for k in range(lo, hi)], axis=1)

    wide = g[8:12].reshape(blocks, slab, d // slab, slab)
    expand_grad = jnp.transpose(wide, (1, 2, 0, 3)).reshape(slab, blocks * d)
    n = o["norm_out"]
    width = norm_gains.shape[1]
    mine = lax.dynamic_slice_in_dim(n, lax.axis_index("frames") * width, width, 1)
    counts = n[8:13, 0]
    branch_rms = jnp.sqrt(counts[:4] / (counts[4] * d))
    return (
        o["result"][None],
        o["tokens_grad"][None],
        o["memory_grad"],
        side(0, 3),
        g[3],
        g[4],
        side(5, 7),
        g[7],
        expand_grad,
        g[12:16].reshape(blocks * slab, d),
        mine[0:4],
        mine[4:8],
        branch_rms,
    )


block_heads = 4


def layer_norm(values, gain_row, shift_row):
    center = values - jnp.mean(values, axis=-1, keepdims=True)
    spread = jnp.mean(center * center, axis=-1, keepdims=True)
    return center * lax.rsqrt(spread + 1e-05) * gain_row + shift_row


def exact_gelu(values):
    return jax.nn.gelu(values, approximate=False)


def matmul(left_side, right_side):
    return jnp.dot(left_side, right_side, preferred_element_type=jnp.float32)


def split_heads(rows):
    return rows.reshape(rows.shape[:-1] + (rows.shape[-1] // HEAD_DIM, HEAD_DIM))


def to_blocks(rows):
    row_count, head_count, head_width = rows.shape
    return rows.reshape(row_count, head_count // block_heads, block_heads, head_width).transpose(
        1, 0, 2, 3
    )


def from_blocks(blocks):
    group_count, row_count, head_count, head_width = blocks.shape
    return blocks.transpose(1, 0, 2, 3).reshape(row_count, group_count * head_count * head_width)


def block_scores(query_block, key_block, allowed):
    factor = query_block.shape[-1] ** (-0.5)
    raw_scores = (
        jnp.einsum("shd,fhd->hsf", query_block, key_block, preferred_element_type=jnp.float32)
        * factor
    )
    return jnp.where(allowed[None], raw_scores, -1e30)


def block_probs(query_block, key_block, allowed, max_block, total_block):
    scores = block_scores(query_block, key_block, allowed)
    shifted = jnp.where(allowed[None], jnp.exp(scores - max_block[..., None]), 0.0)
    return shifted / total_block[..., None]


def block_grads(query_block, key_block, grad_block, probs, grad_probs, row_dot):
    factor = query_block.shape[-1] ** (-0.5)
    score_grad = (probs * (grad_probs - row_dot)).astype(jnp.bfloat16)
    query_grad = (
        jnp.einsum("hsf,fhd->shd", score_grad, key_block, preferred_element_type=jnp.float32)
        * factor
    )
    key_grad = (
        jnp.einsum("hsf,shd->fhd", score_grad, query_block, preferred_element_type=jnp.float32)
        * factor
    )
    value_grad = jnp.einsum(
        "hsf,shd->fhd", probs.astype(jnp.bfloat16), grad_block, preferred_element_type=jnp.float32
    )
    return (query_grad, key_grad, value_grad)


def attend_whole(query_rows, key_rows, value_rows, allowed):

    def one_group(blocks):
        query_block, key_block, value_block = blocks
        scores = block_scores(query_block, key_block, allowed)
        max_block = jnp.max(scores, axis=-1)
        shifted = jnp.where(allowed[None], jnp.exp(scores - max_block[..., None]), 0.0)
        total_block = jnp.sum(shifted, axis=-1)
        weights = (shifted / total_block[..., None]).astype(jnp.bfloat16)
        mixture = jnp.einsum(
            "hsf,fhd->shd", weights, value_block, preferred_element_type=jnp.float32
        )
        return (mixture, max_block, total_block)

    mixture, row_max, totals = lax.map(
        one_group, (to_blocks(query_rows), to_blocks(key_rows), to_blocks(value_rows))
    )
    return (from_blocks(mixture), row_max, totals)


def attend_whole_back(query_rows, key_rows, value_rows, allowed, grad_rows, row_max, totals):

    def one_group(blocks):
        query_block, key_block, value_block, grad_block, max_block, total_block = blocks
        probs = block_probs(query_block, key_block, allowed, max_block, total_block)
        grad_probs = jnp.einsum(
            "shd,fhd->hsf", grad_block, value_block, preferred_element_type=jnp.float32
        )
        row_dot = jnp.sum(probs * grad_probs, axis=-1, keepdims=True)
        return block_grads(query_block, key_block, grad_block, probs, grad_probs, row_dot)

    query_grad, key_grad, value_grad = lax.map(
        one_group,
        (
            to_blocks(query_rows),
            to_blocks(key_rows),
            to_blocks(value_rows),
            to_blocks(grad_rows),
            row_max,
            totals,
        ),
    )
    return (from_blocks(query_grad), from_blocks(key_grad), from_blocks(value_grad))


def cross_stats(query_rows, key_rows, allowed):

    def one_group(blocks):
        query_block, key_block = blocks
        scores = block_scores(query_block, key_block, allowed)
        max_block = jnp.max(scores, axis=-1)
        total_block = jnp.sum(
            jnp.where(allowed[None], jnp.exp(scores - max_block[..., None]), 0.0), axis=-1
        )
        return (max_block, total_block)

    return lax.map(one_group, (to_blocks(query_rows), to_blocks(key_rows)))


def cross_partial(query_rows, key_rows, value_rows, allowed, row_max, totals):

    def one_group(blocks):
        query_block, key_block, value_block, max_block, total_block = blocks
        probs = block_probs(query_block, key_block, allowed, max_block, total_block)
        return jnp.einsum(
            "hsf,fhd->shd",
            probs.astype(jnp.bfloat16),
            value_block,
            preferred_element_type=jnp.float32,
        )

    return from_blocks(
        lax.map(
            one_group,
            (to_blocks(query_rows), to_blocks(key_rows), to_blocks(value_rows), row_max, totals),
        )
    )


def cross_row_dot(query_rows, key_rows, value_rows, allowed, grad_rows, row_max, totals):

    def one_group(blocks):
        query_block, key_block, value_block, grad_block, max_block, total_block = blocks
        probs = block_probs(query_block, key_block, allowed, max_block, total_block)
        grad_probs = jnp.einsum(
            "shd,fhd->hsf", grad_block, value_block, preferred_element_type=jnp.float32
        )
        return jnp.sum(probs * grad_probs, axis=-1)

    return lax.map(
        one_group,
        (
            to_blocks(query_rows),
            to_blocks(key_rows),
            to_blocks(value_rows),
            to_blocks(grad_rows),
            row_max,
            totals,
        ),
    )


def cross_partial_grads(
    query_rows, key_rows, value_rows, allowed, grad_rows, row_max, totals, row_dot
):

    def one_group(blocks):
        query_block, key_block, value_block, grad_block, max_block, total_block, dot_block = blocks
        probs = block_probs(query_block, key_block, allowed, max_block, total_block)
        grad_probs = jnp.einsum(
            "shd,fhd->hsf", grad_block, value_block, preferred_element_type=jnp.float32
        )
        return block_grads(
            query_block, key_block, grad_block, probs, grad_probs, dot_block[..., None]
        )

    query_grad, key_grad, value_grad = lax.map(
        one_group,
        (
            to_blocks(query_rows),
            to_blocks(key_rows),
            to_blocks(value_rows),
            to_blocks(grad_rows),
            row_max,
            totals,
            row_dot,
        ),
    )
    return (from_blocks(query_grad), from_blocks(key_grad), from_blocks(value_grad))


def local(
    tokens,
    memory,
    cotangent,
    self_project,
    self_output,
    cross_query,
    cross_memory,
    cross_output,
    expand,
    contract,
    norm_gains,
    norm_shifts,
    target_length,
    memory_length,
    cross_mask,
):
    gathered = (
        lax.all_gather(self_project, ("dp", "frames"), axis=0, tiled=True),
        lax.all_gather(self_output, ("dp", "frames"), axis=0, tiled=True),
        lax.all_gather(cross_query, ("dp", "frames"), axis=0, tiled=True),
        lax.all_gather(cross_memory, ("dp", "frames"), axis=0, tiled=True),
        lax.all_gather(cross_output, ("dp", "frames"), axis=0, tiled=True),
        lax.all_gather(expand, ("dp", "frames"), axis=0, tiled=True),
        lax.all_gather(contract, ("dp", "frames"), axis=0, tiled=True),
        lax.all_gather(norm_gains, ("dp", "frames"), axis=1, tiled=True),
        lax.all_gather(norm_shifts, ("dp", "frames"), axis=1, tiled=True),
    )
    (
        w_self,
        w_self_out,
        w_query,
        w_memory,
        w_cross_out,
        w_expand,
        w_contract,
        gains_low,
        shifts_low,
    ) = gathered
    gains = gains_low.astype(jnp.float32)
    shifts = shifts_low.astype(jnp.float32)
    model_width = w_self_out.shape[0]
    residual_in = tokens[0]
    length = residual_in.shape[0]
    positions = jnp.arange(length)
    row_valid = positions < target_length[0]
    causal = positions[:, None] >= positions[None, :]
    item_count = memory.shape[0]
    frame_count = memory.shape[1]
    own_item = lax.axis_index("frames")
    normed_one_f, back_one = jax.vjp(layer_norm, residual_in, gains[0], shifts[0])
    normed_one = normed_one_f.astype(jnp.bfloat16)
    joint_rows = matmul(normed_one, w_self).astype(jnp.bfloat16)
    self_queries = split_heads(joint_rows[:, :model_width])
    self_keys = split_heads(joint_rows[:, model_width : 2 * model_width])
    self_values = split_heads(joint_rows[:, 2 * model_width :])
    self_mix, self_max, self_totals = attend_whole(self_queries, self_keys, self_values, causal)
    self_mix_low = self_mix.astype(jnp.bfloat16)
    self_branch = matmul(self_mix_low, w_self_out)
    first_sum = residual_in + self_branch
    normed_two_f, back_two = jax.vjp(layer_norm, first_sum, gains[1], shifts[1])
    normed_two = normed_two_f.astype(jnp.bfloat16)
    cross_queries = matmul(normed_two, w_query).astype(jnp.bfloat16)
    every_query = lax.all_gather(cross_queries[None], "frames", axis=0, tiled=True)
    query_heads = split_heads(every_query)
    frame_start = own_item * frame_count
    local_frames = frame_start + jnp.arange(frame_count)
    local_mask = lax.dynamic_slice_in_dim(cross_mask, frame_start, frame_count, 1)
    frame_ok = (local_frames[None, :] < memory_length[:, None]) & (
        (local_mask == 1) | (local_frames[None, :] == 0)
    )
    memory_rows = matmul(memory.reshape(item_count * frame_count, model_width), w_memory).astype(
        jnp.bfloat16
    )
    memory_rows = memory_rows.reshape(item_count, frame_count, 2 * model_width)
    memory_keys = split_heads(memory_rows[..., :model_width])
    memory_values = split_heads(memory_rows[..., model_width:])

    def item_stats(inputs):
        query_item, key_item, frame_item = inputs
        return cross_stats(
            query_item, key_item, jnp.broadcast_to(frame_item[None, :], (length, frame_count))
        )

    local_max, local_totals = lax.map(item_stats, (query_heads, memory_keys, frame_ok))
    cross_max = lax.pmax(local_max.astype(jnp.bfloat16), "frames").astype(local_max.dtype)
    cross_totals = lax.psum(
        (local_totals * jnp.exp(local_max - cross_max)).astype(jnp.bfloat16), "frames"
    ).astype(jnp.float32)

    def item_partial(inputs):
        query_item, key_item, value_item, frame_item, max_item, total_item = inputs
        allowed = jnp.broadcast_to(frame_item[None, :], (length, frame_count))
        return cross_partial(query_item, key_item, value_item, allowed, max_item, total_item)

    partial_mix = lax.map(
        item_partial, (query_heads, memory_keys, memory_values, frame_ok, cross_max, cross_totals)
    )
    cross_mix = lax.psum_scatter(
        partial_mix.astype(jnp.bfloat16), "frames", scatter_dimension=0, tiled=True
    ).astype(jnp.float32)[0]
    cross_mix_low = cross_mix.astype(jnp.bfloat16)
    cross_branch = matmul(cross_mix_low, w_cross_out)
    second_sum = first_sum + cross_branch
    normed_three_f, back_three = jax.vjp(layer_norm, second_sum, gains[2], shifts[2])
    normed_three = normed_three_f.astype(jnp.bfloat16)
    hidden = matmul(normed_three, w_expand)
    active_f, gelu_back = jax.vjp(exact_gelu, hidden)
    active = active_f.astype(jnp.bfloat16)
    feed_branch = matmul(active, w_contract)
    third_sum = second_sum + feed_branch
    final_rows, back_final = jax.vjp(layer_norm, third_sum, gains[3], shifts[3])
    result = jnp.where(row_valid[:, None], final_rows, 0.0)
    row_weight = row_valid.astype(jnp.float32)[:, None]
    squares = jnp.stack(
        [
            jnp.sum(row_weight * member * member)
            for member in (third_sum, self_branch, cross_branch, feed_branch)
        ]
    )
    squares_all, counted = lax.psum((squares, jnp.sum(row_weight)), ("dp", "frames"))
    branch_rms = jnp.sqrt(squares_all / (counted * model_width))
    grad_result = jnp.where(row_valid[:, None], cotangent[0], 0.0)
    grad_third, gain_grad_three, shift_grad_three = back_final(grad_result)
    feed_low = grad_third.astype(jnp.bfloat16)
    contract_grad = matmul(active.T, feed_low)
    grad_active = matmul(feed_low, w_contract.T)
    grad_hidden = gelu_back(grad_active)[0].astype(jnp.bfloat16)
    expand_grad = matmul(normed_three.T, grad_hidden)
    grad_normed_three = matmul(grad_hidden, w_expand.T)
    grad_second_part, gain_grad_two, shift_grad_two = back_three(grad_normed_three)
    grad_second = grad_third + grad_second_part
    cross_low = grad_second.astype(jnp.bfloat16)
    cross_output_grad = matmul(cross_mix_low.T, cross_low)
    grad_cross_mix = matmul(cross_low, w_cross_out.T).astype(jnp.bfloat16)
    every_grad = split_heads(lax.all_gather(grad_cross_mix[None], "frames", axis=0, tiled=True))

    def item_dot(inputs):
        query_item, key_item, value_item, frame_item, grad_item, max_item, total_item = inputs
        allowed = jnp.broadcast_to(frame_item[None, :], (length, frame_count))
        return cross_row_dot(
            query_item, key_item, value_item, allowed, grad_item, max_item, total_item
        )

    local_dot = lax.map(
        item_dot,
        (query_heads, memory_keys, memory_values, frame_ok, every_grad, cross_max, cross_totals),
    )
    row_dot = lax.psum(local_dot.astype(jnp.bfloat16), "frames").astype(jnp.float32)

    def item_grads(inputs):
        query_item, key_item, value_item, frame_item, grad_item, max_item, total_item, dot_item = (
            inputs
        )
        allowed = jnp.broadcast_to(frame_item[None, :], (length, frame_count))
        return cross_partial_grads(
            query_item, key_item, value_item, allowed, grad_item, max_item, total_item, dot_item
        )

    query_parts, key_parts, value_parts = lax.map(
        item_grads,
        (
            query_heads,
            memory_keys,
            memory_values,
            frame_ok,
            every_grad,
            cross_max,
            cross_totals,
            row_dot,
        ),
    )
    query_grad = lax.psum_scatter(
        query_parts.astype(jnp.bfloat16), "frames", scatter_dimension=0, tiled=True
    ).astype(jnp.float32)[0]
    memory_low = (
        jnp.concatenate([key_parts, value_parts], axis=2)
        .astype(jnp.bfloat16)
        .reshape(item_count * frame_count, 2 * model_width)
    )
    cross_memory_grad = matmul(memory.reshape(item_count * frame_count, model_width).T, memory_low)
    memory_grad = matmul(memory_low, w_memory.T).reshape(item_count, frame_count, model_width)
    query_low = query_grad.astype(jnp.bfloat16)
    cross_query_grad = matmul(normed_two.T, query_low)
    grad_normed_two = matmul(query_low, w_query.T)
    grad_first_part, gain_grad_one, shift_grad_one = back_two(grad_normed_two)
    grad_first = grad_second + grad_first_part
    self_low = grad_first.astype(jnp.bfloat16)
    self_output_grad = matmul(self_mix_low.T, self_low)
    grad_self_mix = matmul(self_low, w_self_out.T).astype(jnp.bfloat16)
    self_query_grad, self_key_grad, self_value_grad = attend_whole_back(
        self_queries,
        self_keys,
        self_values,
        causal,
        split_heads(grad_self_mix),
        self_max,
        self_totals,
    )
    joint_grad = jnp.concatenate([self_query_grad, self_key_grad, self_value_grad], axis=1).astype(
        jnp.bfloat16
    )
    self_project_grad = matmul(normed_one.T, joint_grad)
    grad_normed_one = matmul(joint_grad, w_self.T)
    grad_input_part, gain_grad_zero, shift_grad_zero = back_one(grad_normed_one)
    tokens_grad = grad_first + grad_input_part
    gain_grads = jnp.stack([gain_grad_zero, gain_grad_one, gain_grad_two, gain_grad_three])
    shift_grads = jnp.stack([shift_grad_zero, shift_grad_one, shift_grad_two, shift_grad_three])
    reduced = (
        lax.psum_scatter(self_project_grad, ("dp", "frames"), scatter_dimension=0, tiled=True),
        lax.psum_scatter(self_output_grad, ("dp", "frames"), scatter_dimension=0, tiled=True),
        lax.psum_scatter(cross_query_grad, ("dp", "frames"), scatter_dimension=0, tiled=True),
        lax.psum_scatter(cross_memory_grad, ("dp", "frames"), scatter_dimension=0, tiled=True),
        lax.psum_scatter(cross_output_grad, ("dp", "frames"), scatter_dimension=0, tiled=True),
        lax.psum_scatter(expand_grad, ("dp", "frames"), scatter_dimension=0, tiled=True),
        lax.psum_scatter(contract_grad, ("dp", "frames"), scatter_dimension=0, tiled=True),
        lax.psum_scatter(gain_grads, ("dp", "frames"), scatter_dimension=1, tiled=True),
        lax.psum_scatter(shift_grads, ("dp", "frames"), scatter_dimension=1, tiled=True),
    )
    (
        project_part,
        output_part,
        query_part,
        memory_part,
        cross_out_part,
        expand_part,
        contract_part,
        gains_part,
        shifts_part,
    ) = reduced
    return (
        result[None],
        tokens_grad[None],
        memory_grad,
        project_part,
        output_part,
        query_part,
        memory_part,
        cross_out_part,
        expand_part,
        contract_part,
        gains_part,
        shifts_part,
        branch_rms,
    )


def solution(mesh):
    fits = (mesh.shape["dp"], mesh.shape["frames"]) == (2 * Z_CHIPS, 4)
    return jax.shard_map(
        local_fused if fits else local,
        mesh=mesh,
        in_specs=(
            P(("dp", "frames"), None, None),
            P("dp", "frames", None),
            P(("dp", "frames"), None, None),
            P(("dp", "frames"), None),
            P(("dp", "frames"), None),
            P(("dp", "frames"), None),
            P(("dp", "frames"), None),
            P(("dp", "frames"), None),
            P(("dp", "frames"), None),
            P(("dp", "frames"), None),
            P(None, ("dp", "frames")),
            P(None, ("dp", "frames")),
            P(("dp", "frames")),
            P("dp"),
            P("dp", None),
        ),
        out_specs=(
            P(("dp", "frames"), None, None),
            P(("dp", "frames"), None, None),
            P("dp", "frames", None),
            P(("dp", "frames"), None),
            P(("dp", "frames"), None),
            P(("dp", "frames"), None),
            P(("dp", "frames"), None),
            P(("dp", "frames"), None),
            P(("dp", "frames"), None),
            P(("dp", "frames"), None),
            P(None, ("dp", "frames")),
            P(None, ("dp", "frames")),
            P(),
        ),
        check_vma=False,
    )
```

time: 1790 us -> 411 us (0.23)
  waiting for transfers between devices: 1250 us -> 0 us
  Pallas kernels: 192 us -> 365 us
  matrix products: 116 us -> 0 us
  local copies, waits for them, and re-layouts: 146 us -> 34.7 us
  blocking collectives: 50.7 us -> 0 us
    reduce_scatter x7 -> x0, waiting for transfers between devices: 956 us -> none  [the longest x1 185 us: local_fast(): lax.psum_scatter(natural(contract_grad, contract.shape[0] // expand.shape...]
    unnamed x14 -> x0, waiting for transfers between devices: 298 us -> none
    pallas_call x1, Pallas kernels: 192 us -> 365 us  [fused(): pl.pallas_call(kernel, out_shape=[jax.ShapeDtypeStruct(s, t) for s, t, _...]
    dot_general x114 -> x0, matrix products: 116 us -> none  [the longest x14 68.8 us: matmul(): return jnp.dot(left_side, right_side, preferred_element_type=jnp.float32)]
    psum x1 -> x0, blocking collectives: 39.7 us -> none  [local_fast(): total = lax.psum(o['sq'][:5, 0], ('dp', 'frames'))]
    slice x13 -> x3, local copies, waits for them, and re-layouts: 42.7 us -> 3.62 us  [the longest x1 1.4 us: local_fused(): mine[4:8]]
  transfers between devices with their start and end apart: 11 -> 0, of which waited for: 10 -> 0; matrix products, arithmetic and copies ran while one was open for 6% -> 0% of each run, Pallas kernels for 0% -> 0%
where the time goes in v2:
time: 411 us; the launch traced here: 406 us
  Pallas kernels  365 us (89%)
  local copies, waits for them, and re-layouts  34.7 us (8%)
  other arithmetic  4.3 us (1%)
    pallas_call x1, Pallas kernels, fused(): pl.pallas_call(kernel, out_shape=[jax.ShapeDtypeStruct(s, t) for s, t, _...  365 us
    unnamed x21, local copies, waits for them, and re-layouts  12.5 us

profile of v2, /device:TPU:0, one launch (start us, length us, event | category | flops | bytes accessed | tf_op | source)
XLA Modules:
  0.0 406.1 jit_solution(11044776015314769336)
XLA Ops:
  1.3 0.7 pad_maximum_fusion.2
  2.0 0.8 fusion.4
  2.8 0.6 pad.9.refs_6_
  3.4 0.2 dynamic_update_slice.3.refs_5_
  3.6 0.0 copy-start.5
  3.6 0.9 fusion
  4.6 0.8 bitcast_dynamic-update-slice_fusion.2
  5.4 0.8 bitcast_dynamic-update-slice_fusion.1
  6.3 0.9 fusion.1
  7.2 0.8 bitcast_dynamic-update-slice_fusion
  8.0 1.7 reshape.73
  9.8 0.0 copy-start.4
  9.8 0.2 copy.39
  10.0 0.0 copy-done.5
  10.0 1.1 reshape.74
  11.1 0.0 copy-start.1
  11.1 4.3 %pad.8 = bf16[4,384,1024]{2,1,0:T(8,128)(2,1)} pad(bf16[4,376,1024]{2,1,0:T(8,128)(2,1)} %param.16, bf16[]{:T(256)} %constant.11.clone.1), padding=0_0x0_8x0_0 | pad | bytes 6225922 | tf_op jit(solution)/shard_map/jit(_pad)/pad | solution.py:1069
  15.5 0.0 copy-done.1
  15.5 364.8 %shard_map.246 = (f32[128,1024]{1,0:T(8,128)}, f32[128,1024]{1,0:T(8,128)}, f32[4,376,1024]{2,1,0:T(8,128)}, f32[16,32,1024]{2,1,0:T(8,128)}, f32[16,128]{1,0:T(8,128)}) custom-call(s32[1]{0:T(128)S(6)} %copy.50.refs_0_, f32[128,1024]{1,0:T(8,128)} %bitcast.57, f32[128,1024]{1,0:T(8,128)} %bitcast.58, bf16[4,3,2,2,32,1024]{5,4,3,2,1,0:T(8,128)(2,1)} %bitcast.54, ...), custom_call_target="tpu_custom_call" | custom-call | tf_op jit(solution)/shard_map/pallas_call | solution.py:1000
  380.3 1.3 slice.60
  382.3 1.3 sqrt_reduce_fusion
  383.6 1.4 fusion.6
  385.0 2.1 slice_bitcast_fusion
  387.1 0.9 fusion.5
  388.0 0.7 pad_maximum_fusion.1
  388.7 0.8 pad_maximum_fusion
  389.5 0.7 reshape.76
  390.2 3.1 copy.33
  393.3 4.5 %reshape.77 = f32[32,4096]{1,0:T(8,128)} reshape(f32[32,32,4,32]{3,2,1,0:T(4,128)} %copy.33) | data formatting | bytes 1048576 | tf_op jit(solution)/shard_map/reshape | solution.py:1090
  397.8 0.8 copy.51
  398.6 0.8 copy.52
  399.4 6.5 %copy.53 = f32[4,376,1024]{2,1,0:T(8,128)} copy(f32[4,376,1024]{2,1,0:T(8,128)} %get-tuple-element.50) | data formatting | bytes 12320768
  (12 shorter events, 0.1 us)
Async XLA Ops:
  3.6 6.3 %copy-start.5 = (bf16[32,128]{1,0:T(8,128)(2,1)}, bf16[32,128]{1,0:T(8,128)(2,1)S(1)}, u32[]{:S(2)}) copy-start(bf16[32,128]{1,0:T(8,128)(2,1)S(1)} %dynamic_update_slice.3.refs_5_) | copy-start | bytes 24580
  9.8 1.3 copy-start.4
  11.1 4.3 %copy-start.1 = (bf16[16,32,1024]{2,1,0:T(8,128)(2,1)}, bf16[16,32,1024]{2,1,0:T(8,128)(2,1)S(1)}, u32[]{:S(2)}) copy-start(bf16[16,32,1024]{2,1,0:T(8,128)(2,1)S(1)} %constant_dynamic-update-slice_fusion.refs_4_) | copy-start | bytes 3145732
  380.3 6.8 %copy-start = (f32[16,32,1024]{2,1,0:T(8,128)S(1)}, f32[16,32,1024]{2,1,0:T(8,128)}, u32[]{:S(2)}) copy-start(f32[16,32,1024]{2,1,0:T(8,128)} %get-tuple-element.21) | copy-start | bytes 6291460
  393.3 4.5 %copy-start.3 = (f32[128,1024]{1,0:T(8,128)S(1)}, f32[128,1024]{1,0:T(8,128)}, u32[]{:S(2)}) copy-start(f32[128,1024]{1,0:T(8,128)} %get-tuple-element.18) | copy-start | bytes 1572868
  393.3 5.3 %copy-start.2 = (f32[128,1024]{1,0:T(8,128)S(1)}, f32[128,1024]{1,0:T(8,128)}, u32[]{:S(2)}) copy-start(f32[128,1024]{1,0:T(8,128)} %get-tuple-element.19) | copy-start | bytes 1572868
